TPU v7x, 128 devices: a whole 4x4x4 slice. The times are simulated.
128 devices in a mesh: lap: 4 (over x), space: 32 (over y, z, core).
Axes of the slice: x: 4, y: 4, z: 4, core: 2. Of those that a mesh axis runs over, the one named last changes fastest.
Arguments:
- slowness: float32 [64, 512, 128], P('space'), may hold values from 0.25 to 1
- damping: float32 [16], P('lap'), may hold values from 0.2 to 1.5
- src_index: int32 [32768], P('space'), may hold values from 0 to 4194303, as said below
- src_amp: float32 [16, 32768], P('lap', 'space'), may hold values from -12 to 12
- rec_index: int32 [32768], P('space'), may hold values from 0 to 4194303, as said below
- observed: float32 [16, 32768], P('lap', 'space'), may hold values from -0.6 to 0.6
- dual: float32 [3, 64, 512, 128], P(None, 'space', 'lap'), may hold values from -2 to 2
Outputs:
- model: float32 [64, 512, 128], P('space', 'lap')
- dual_next: float32 [3, 64, 512, 128], P(None, 'space', 'lap')
Inputs may be any that keep to these rules, and one draw needn't show every extreme that they name: `src_index`: entry k lies in the slab of grid cells whose first index is from (k // 1024) * 2 to (k // 1024) * 2 + 1; cells may repeat. `rec_index`: entry k lies in the slab of grid cells whose first index is from (k // 1024) * 2 to (k // 1024) * 2 + 1; cells may repeat.
All inputs are finite; a program needn't handle non-finite values.
Results may differ from a plain program's by a relative error of at most 0.0001.
Values sent between devices are 32-bit elements; how exact they have to be, the bound alone decides.
No kernel may reach another device: no remote copies, remote signals or barrier semaphores. Data moves between devices by JAX's collectives and lax.ppermute only.
A program may use at most 192 MiB of HBM per device.

v0:
```python
import jax
import jax.numpy as jnp
from jax import lax
from jax.sharding import PartitionSpec as P

ITERS = 3


dual_step = 0.5
primal_step = 0.2
tv_weight = 0.5


def with_halo(block, sides, width):
    for axis, dim in sides:
        count = lax.axis_size(axis)
        forward = [(i, i + 1) for i in range(count - 1)]
        backward = [(target, source) for source, target in forward]
        low = lax.ppermute(
            lax.slice_in_dim(block, block.shape[dim] - width, None, axis=dim), axis, forward
        )
        high = lax.ppermute(lax.slice_in_dim(block, 0, width, axis=dim), axis, backward)
        block = jnp.concatenate([low, block, high], axis=dim)
    return block


def shifted(x, axis, by):
    peers = lax.axis_size(axis)
    pairs = [(i, i + by) for i in range(peers) if 0 <= i + by < peers]
    return lax.ppermute(x, axis, pairs)


def spread(vector):
    return vector[:, None, None, None]


def operate(field, diagonal):
    padded = with_halo(field, (("space", 1),), 1)
    padded_yz = jnp.pad(field, ((0, 0), (0, 0), (1, 1), (1, 1)))
    beside = padded[:, 2:] + padded[:, :-2]
    beside = beside + padded_yz[:, :, 2:, 1:-1] + padded_yz[:, :, :-2, 1:-1]
    beside = beside + padded_yz[:, :, 1:-1, 2:] + padded_yz[:, :, 1:-1, :-2]
    return diagonal * field - beside


def cell_sum(left_field, right_field):
    return jnp.sum(left_field * right_field, axis=(1, 2, 3))


def energy_of(residual, precon):
    return lax.psum(cell_sum(residual, precon), "space")


def precond_solve(right_side, diagonal):
    iterate = jnp.zeros_like(right_side)
    residual = right_side
    precon = residual / diagonal
    direction = precon
    energy = energy_of(residual, precon)
    for iteration in range(ITERS):
        applied = operate(direction, diagonal)
        stride = energy / lax.psum(cell_sum(direction, applied), "space")
        iterate = iterate + spread(stride) * direction
        if iteration + 1 < ITERS:
            residual = residual - spread(stride) * applied
            precon = residual / diagonal
            energy_new = energy_of(residual, precon)
            direction = precon + spread(energy_new / energy) * direction
            energy = energy_new
    return iterate


def on_device(slowness, damping, src_index, src_amp, rec_index, observed, dual):
    width_x, rows_y, depth_z = slowness.shape
    slab_cells = width_x * rows_y * depth_z
    space_pos = lax.axis_index("space")
    lap_pos = lax.axis_index("lap")
    offset = space_pos * slab_cells
    src_local = src_index - offset
    rec_local = rec_index - offset
    constants = damping.shape[0]
    squared = damping * damping
    diagonal = 6.0 + spread(squared) * slowness[None]
    source = jnp.zeros((constants, slab_cells), jnp.float32).at[:, src_local].add(src_amp)
    wavefield = precond_solve(source.reshape(constants, width_x, rows_y, depth_z), diagonal)
    misfit = wavefield.reshape(constants, slab_cells)[:, rec_local] - observed
    adjoint_source = jnp.zeros((constants, slab_cells), jnp.float32).at[:, rec_local].add(misfit)
    adjoint = precond_solve(adjoint_source.reshape(constants, width_x, rows_y, depth_z), diagonal)
    partial_grad = -jnp.sum(spread(squared) * wavefield * adjoint, axis=0)
    band_rows = rows_y // lax.axis_size("lap")
    start_y = lap_pos * band_rows
    summed = lax.psum(partial_grad, "lap")
    own_grad = lax.dynamic_slice_in_dim(summed, start_y, band_rows, 1)
    power_sum = lax.psum(jnp.sum(own_grad * own_grad), ("lap", "space"))
    total_cells = slab_cells * lax.axis_size("space")
    scaled = own_grad / jnp.sqrt(power_sum / total_cells + 1e-06)
    padded_model = jnp.pad(slowness, ((0, 0), (0, 1), (0, 0)))
    window = lax.dynamic_slice_in_dim(padded_model, start_y, band_rows + 1, 1)
    own_model = window[:, :band_rows]
    x_glob = space_pos * width_x + jnp.arange(width_x, dtype=jnp.int32)
    last_x = (x_glob == width_x * lax.axis_size("space") - 1)[:, None, None]
    y_glob = start_y + jnp.arange(band_rows, dtype=jnp.int32)
    last_y = (y_glob == rows_y - 1)[None, :, None]
    following = shifted(own_model[:1], "space", -1)
    step_x = jnp.where(last_x, 0.0, jnp.concatenate([own_model[1:], following], 0) - own_model)
    step_y = jnp.where(last_y, 0.0, window[:, 1:] - own_model)
    step_z = jnp.concatenate(
        [own_model[:, :, 1:] - own_model[:, :, :-1], jnp.zeros_like(own_model[:, :, :1])], 2
    )
    dual_trial = dual + dual_step * jnp.stack([step_x, step_y, step_z])
    magnitude = jnp.sqrt(jnp.sum(dual_trial * dual_trial, axis=0))
    dual_next = dual_trial / jnp.maximum(1.0, magnitude / tv_weight)
    comp_x = jnp.where(last_x, 0.0, dual_next[0])
    comp_y = jnp.where(last_y, 0.0, dual_next[1])
    comp_z = jnp.concatenate([dual_next[2][:, :, :-1], jnp.zeros_like(dual_next[2][:, :, :1])], 2)
    prior_x = shifted(comp_x[-1:], "space", 1)
    back_x = jnp.concatenate([prior_x, comp_x[:-1]], 0) - comp_x
    prior_y = shifted(comp_y[:, -1:], "lap", 1)
    back_y = jnp.concatenate([prior_y, comp_y[:, :-1]], 1) - comp_y
    back_z = jnp.concatenate([jnp.zeros_like(comp_z[:, :, :1]), comp_z[:, :, :-1]], 2) - comp_z
    model = own_model - primal_step * (scaled + back_x + back_y + back_z)
    return (model, dual_next)


def solution(mesh):
    in_specs = (
        P("space", None, None),
        P("lap"),
        P("space"),
        P("lap", "space"),
        P("space"),
        P("lap", "space"),
        P(None, "space", "lap", None),
    )
    out_specs = (P("space", "lap", None), P(None, "space", "lap", None))
    return jax.shard_map(
        on_device, mesh=mesh, in_specs=in_specs, out_specs=out_specs, check_vma=False
    )
```

profile of v0, /device:TPU:1, one launch (start us, length us, event | category | flops | bytes accessed | tf_op | source)
XLA Modules:
  0.0 1182.7 jit_solution(15295976219730734389)
XLA Ops:
  8.7 3.8 sort
  13.4 42.5 %scatter_custom_fusion = f32[4,131072]{0,1:T(8,128)} fusion(s32[1024]{0:T(1024)S(1)} %get-tuple-element.2, f32[]{:T(128)} %constant.20.clone.1, f32[1024,4]{1,0:T(8,128)S(1)} %copy.18, s32[1024]{0:T(1024)S(1)} %broadcast_clamp_fusion.2), kind=kCustom, calls=%fused_computation.7 | custom fusion | flops 4096 | bytes 2097156 | tf_op jit(solution)/shard_map/scatter-add | solution.py:84
  55.9 35.6 %copy.21 = f32[4,2,512,128]{3,2,1,0:T(8,128)S(1)} copy(f32[4,2,512,128]{0,3,2,1:T(8,128)} %bitcast.2) | data formatting | bytes 4194304 | tf_op jit(solution)/shard_map/reshape | solution.py:85
  93.8 3.3 collective-permute-start
  97.1 3.5 collective-permute-start.1
  100.7 34.5 %copy.20 = f32[4,131072]{1,0:T(4,128)} copy(f32[4,131072]{0,1:T(8,128)} %scatter_custom_fusion) | data formatting | bytes 4194304 | tf_op jit(solution)/shard_map/scatter-add | solution.py:84
  135.2 3.0 fusion.50
  138.2 4.0 multiply_reduce_fusion.8
  142.2 63.5 %all-reduce.10 = (f32[4]{0:T(128)S(1)}, f32[4]{0:T(128)S(1)}) all-reduce(f32[4]{0:T(128)S(1)} %fusion.50, f32[4]{0:T(128)S(1)} %get-tuple-element.22), channel_id=1, replica_groups=mesh['lap'=4,'space'=32] {'space'}, use_global_device_ids=true, to_apply=%region_2.0 | all-reduce | flops 8 | bytes 64 | tf_op jit(solution)/shard_map/psum | solution.py:51
  205.8 3.5 multiply_reduce_fusion.7
  209.3 66.6 %psum.100 = f32[4]{0:T(128)S(1)} all-reduce(f32[4]{0:T(128)S(1)} %get-tuple-element.20), channel_id=1, replica_groups=mesh['lap'=4,'space'=32] {'space'}, use_global_device_ids=true, to_apply=%region_6.7 | all-reduce | flops 4 | bytes 32 | tf_op jit(solution)/shard_map/psum | solution.py:51
  280.7 3.0 collective-permute-start.3
  283.7 10.5 collective-permute-done.2
  298.2 59.3 %psum.101 = f32[4]{0:T(128)S(1)} all-reduce(f32[4]{0:T(128)S(1)} %get-tuple-element.18), channel_id=1, replica_groups=mesh['lap'=4,'space'=32] {'space'}, use_global_device_ids=true, to_apply=%region_8.9 | all-reduce | flops 4 | bytes 32 | tf_op jit(solution)/shard_map/psum | solution.py:62
  357.6 2.9 multiply_reduce_fusion.5
  360.5 65.9 %psum.102 = f32[4]{0:T(128)S(1)} all-reduce(f32[4]{0:T(128)S(1)} %multiply_reduce_fusion.5), channel_id=1, replica_groups=mesh['lap'=4,'space'=32] {'space'}, use_global_device_ids=true, to_apply=%region_10.11 | all-reduce | flops 4 | bytes 32 | tf_op jit(solution)/shard_map/psum | solution.py:51
  426.4 3.5 multiply_add_fusion.3
  434.4 3.0 collective-permute-start.5
  437.4 3.8 sort.1
  441.2 7.1 collective-permute-done.4
  449.5 7.5 fusion.53
  457.2 59.3 %psum.103 = f32[4]{0:T(128)S(1)} all-reduce(f32[4]{0:T(128)S(1)} %fusion.53), channel_id=1, replica_groups=mesh['lap'=4,'space'=32] {'space'}, use_global_device_ids=true, to_apply=%region_12.13 | all-reduce | flops 4 | bytes 32 | tf_op jit(solution)/shard_map/psum | solution.py:62
  516.6 4.2 multiply_add_fusion.2
  520.8 31.2 %copy.23 = f32[4,2,512,128]{0,3,2,1:T(8,128)} copy(f32[4,2,512,128]{3,2,1,0:T(8,128)} %multiply_add_fusion.2) | data formatting | bytes 4194304 | tf_op jit(solution)/shard_map/add | solution.py:63
  552.0 10.5 gather_fusion
  562.6 42.5 %scatter_custom_fusion.1 = f32[4,131072]{0,1:T(8,128)} fusion(s32[1024]{0:T(1024)S(1)} %get-tuple-element.4, f32[]{:T(128)} %constant.20.clone.1, f32[1024,4]{1,0:T(8,128)S(1)} %fusion.60, s32[1024]{0:T(1024)S(1)} %broadcast_clamp_fusion.1), kind=kCustom, calls=%fused_computation.5 | custom fusion | flops 4096 | bytes 2097156 | tf_op jit(solution)/shard_map/scatter-add | solution.py:87
  605.0 35.4 %copy.27 = f32[4,2,512,128]{3,2,1,0:T(8,128)S(1)} copy(f32[4,2,512,128]{0,3,2,1:T(8,128)} %bitcast.6) | data formatting | bytes 4194304 | tf_op jit(solution)/shard_map/reshape | solution.py:88
  642.9 5.8 collective-permute-start.6
  650.6 34.5 %copy.26 = f32[4,131072]{1,0:T(4,128)} copy(f32[4,131072]{0,1:T(8,128)} %scatter_custom_fusion.1) | data formatting | bytes 4194304 | tf_op jit(solution)/shard_map/scatter-add | solution.py:87
  685.1 3.0 fusion.51
  688.2 4.0 multiply_reduce_fusion.4
  692.1 63.5 %all-reduce.9 = (f32[4]{0:T(128)S(1)}, f32[4]{0:T(128)S(1)}) all-reduce(f32[4]{0:T(128)S(1)} %fusion.51, f32[4]{0:T(128)S(1)} %get-tuple-element.14), channel_id=1, replica_groups=mesh['lap'=4,'space'=32] {'space'}, use_global_device_ids=true, to_apply=%region_15.16 | all-reduce | flops 8 | bytes 64 | tf_op jit(solution)/shard_map/psum | solution.py:51
  755.6 3.5 multiply_reduce_fusion.3
  759.1 62.7 %psum.106 = f32[4]{0:T(128)S(1)} all-reduce(f32[4]{0:T(128)S(1)} %get-tuple-element.12), channel_id=1, replica_groups=mesh['lap'=4,'space'=32] {'space'}, use_global_device_ids=true, to_apply=%region_19.20 | all-reduce | flops 4 | bytes 32 | tf_op jit(solution)/shard_map/psum | solution.py:51
  826.7 3.0 collective-permute-start.9
  829.7 10.5 collective-permute-done.8
  844.2 59.3 %psum.107 = f32[4]{0:T(128)S(1)} all-reduce(f32[4]{0:T(128)S(1)} %get-tuple-element.10), channel_id=1, replica_groups=mesh['lap'=4,'space'=32] {'space'}, use_global_device_ids=true, to_apply=%region_21.22 | all-reduce | flops 4 | bytes 32 | tf_op jit(solution)/shard_map/psum | solution.py:62
  903.5 2.9 multiply_reduce_fusion.1
  906.4 65.9 %psum.108 = f32[4]{0:T(128)S(1)} all-reduce(f32[4]{0:T(128)S(1)} %multiply_reduce_fusion.1), channel_id=1, replica_groups=mesh['lap'=4,'space'=32] {'space'}, use_global_device_ids=true, to_apply=%region_23.24 | all-reduce | flops 4 | bytes 32 | tf_op jit(solution)/shard_map/psum | solution.py:51
  972.3 3.5 multiply_add_fusion
  980.5 3.0 collective-permute-start.11
  986.0 8.9 collective-permute-done.12
  995.6 3.3 fusion.52
  998.9 60.0 %psum.109 = f32[4]{0:T(128)} all-reduce(f32[4]{0:T(128)} %fusion.52), channel_id=1, replica_groups=mesh['lap'=4,'space'=32] {'space'}, use_global_device_ids=true, to_apply=%region_25.26 | all-reduce | flops 4 | bytes 32 | tf_op jit(solution)/shard_map/psum | solution.py:62
  1059.5 3.9 multiply_reduce_fusion
  1064.5 3.1 collective-permute-start.14
  1069.7 35.1 %all-reduce.13.cloned.1.call-done = f32[2,512,128]{2,1,0:T(8,128)} async-done(((f32[2,512,128]{2,1,0:T(8,128)}), f32[2,512,128]{2,1,0:T(8,128)}) %all-reduce.13.cloned.1.call-update) | async-done | bytes 524304 | tf_op jit(solution)/shard_map/psum | solution.py:92
  1106.4 66.9 %psum.111 = f32[]{:T(128)} all-reduce(f32[]{:T(128)} %multiply_reduce_fusion.10), channel_id=1, replica_groups=mesh['lap'=4,'space'=32] {'lap','space'}, use_global_device_ids=true, to_apply=%region_29.30 | all-reduce | flops 1 | bytes 8 | tf_op jit(solution)/shard_map/psum | solution.py:94
  (99 shorter events, 47.6 us)
Async XLA Ops:
  7.2 1097.6 %all-reduce.13.cloned.1.call-start = ((), (), s32[]{:S(2)}) async-start(), calls=%async_computation | async-start | bytes 1048576 | tf_op jit(solution)/shard_map/psum | solution.py:92
  55.9 35.6 %copy-start = (f32[2,512,128]{2,1,0:T(8,128)S(1)}, f32[2,512,128]{2,1,0:T(8,128)}, u32[]{:S(2)}) copy-start(f32[2,512,128]{2,1,0:T(8,128)} %param.7) | copy-start | bytes 1572868
  91.8 2.0 copy-start.6
  93.8 44.4 %collective-permute-start = (f32[4,1,512,128]{3,2,1,0:T(8,128)}, f32[4,1,512,128]{3,2,1,0:T(8,128)}, u32[]{:S(2)}, u32[]{:S(2)}) collective-permute-start(f32[4,1,512,128]{3,2,1,0:T(8,128)} %get-tuple-element.34), channel_id=1, source_target_pairs={{1,0},{2,1},{3,2},{4,3},{5,4},{6,5},{7,6},{8,7},{9,8},{10,9},{11,1... | collective-permute-start | bytes 3145736 | tf_op jit(solution)/shard_map/ppermute | solution.py:22
  97.1 41.1 %collective-permute-start.1 = (f32[4,1,512,128]{3,2,1,0:T(8,128)}, f32[4,1,512,128]{3,2,1,0:T(8,128)}, u32[]{:S(2)}, u32[]{:S(2)}) collective-permute-start(f32[4,1,512,128]{3,2,1,0:T(8,128)} %get-tuple-element.35), channel_id=1, source_target_pairs={{0,1},{1,2},{2,3},{3,4},{4,5},{5,6},{6,7},{7,8},{8,9},{9,10},{10,1... | collective-permute-start | bytes 3145736 | tf_op jit(solution)/shard_map/ppermute | solution.py:19
  135.2 3.0 copy-start.7
  278.0 17.5 %copy-start.2 = (f32[4,2,512,128]{3,2,1,0:T(8,128)}, f32[4,2,512,128]{3,2,1,0:T(8,128)S(1)}, u32[]{:S(2)}) copy-start(f32[4,2,512,128]{3,2,1,0:T(8,128)S(1)} %multiply_add_fusion.4) | copy-start | bytes 6291460
  278.2 16.1 %collective-permute-start.2 = (f32[4,1,512,128]{3,2,1,0:T(8,128)S(1)}, f32[4,1,512,128]{3,2,1,0:T(8,128)S(1)}, u32[]{:S(2)}, u32[]{:S(2)}) collective-permute-start(f32[4,1,512,128]{3,2,1,0:T(8,128)S(1)} %get-tuple-element.32), channel_id=1, source_target_pairs={{1,0},{2,1},{3,2},{4,3},{5,4},{6,5},{7,6},{8,7},{9,8},{10,9},{11,1... | collective-permute-start | bytes 3145736 | tf_op jit(solution)/shard_map/ppermute | solution.py:22
  280.7 14.7 %collective-permute-start.3 = (f32[4,1,512,128]{3,2,1,0:T(8,128)S(1)}, f32[4,1,512,128]{3,2,1,0:T(8,128)S(1)}, u32[]{:S(2)}, u32[]{:S(2)}) collective-permute-start(f32[4,1,512,128]{3,2,1,0:T(8,128)S(1)} %get-tuple-element.33), channel_id=1, source_target_pairs={{0,1},{1,2},{2,3},{3,4},{4,5},{5,6},{6,7},{7,8},{8,9},{9,10},{10,1... | collective-permute-start | bytes 3145736 | tf_op jit(solution)/shard_map/ppermute | solution.py:19
  429.8 2.0 copy-start.5
  431.9 16.4 %collective-permute-start.4 = (f32[4,1,512,128]{3,2,1,0:T(8,128)}, f32[4,1,512,128]{3,2,1,0:T(8,128)}, u32[]{:S(2)}, u32[]{:S(2)}) collective-permute-start(f32[4,1,512,128]{3,2,1,0:T(8,128)} %get-tuple-element.30), channel_id=1, source_target_pairs={{1,0},{2,1},{3,2},{4,3},{5,4},{6,5},{7,6},{8,7},{9,8},{10,9},{11,1... | collective-permute-start | bytes 3145736 | tf_op jit(solution)/shard_map/ppermute | solution.py:22
  434.4 15.1 %collective-permute-start.5 = (f32[4,1,512,128]{3,2,1,0:T(8,128)}, f32[4,1,512,128]{3,2,1,0:T(8,128)}, u32[]{:S(2)}, u32[]{:S(2)}) collective-permute-start(f32[4,1,512,128]{3,2,1,0:T(8,128)} %get-tuple-element.31), channel_id=1, source_target_pairs={{0,1},{1,2},{2,3},{3,4},{4,5},{5,6},{6,7},{7,8},{8,9},{9,10},{10,1... | collective-permute-start | bytes 3145736 | tf_op jit(solution)/shard_map/ppermute | solution.py:19
  441.2 15.8 %copy-start.12 = (f32[4,1024]{1,0:T(4,128)S(1)}, f32[4,1024]{1,0:T(4,128)}, u32[]{:S(2)}) copy-start(f32[4,1024]{1,0:T(4,128)} %param.12) | copy-start | bytes 49156
  640.8 2.1 copy-start.8
  642.9 45.3 %collective-permute-start.6 = (f32[4,1,512,128]{3,2,1,0:T(8,128)}, f32[4,1,512,128]{3,2,1,0:T(8,128)}, u32[]{:S(2)}, u32[]{:S(2)}) collective-permute-start(f32[4,1,512,128]{3,2,1,0:T(8,128)} %get-tuple-element.28), channel_id=1, source_target_pairs={{1,0},{2,1},{3,2},{4,3},{5,4},{6,5},{7,6},{8,7},{9,8},{10,9},{11,1... | collective-permute-start | bytes 3145736 | tf_op jit(solution)/shard_map/ppermute | solution.py:22
  648.7 39.5 %collective-permute-start.7 = (f32[4,1,512,128]{3,2,1,0:T(8,128)}, f32[4,1,512,128]{3,2,1,0:T(8,128)}, u32[]{:S(2)}, u32[]{:S(2)}) collective-permute-start(f32[4,1,512,128]{3,2,1,0:T(8,128)} %get-tuple-element.29), channel_id=1, source_target_pairs={{0,1},{1,2},{2,3},{3,4},{4,5},{5,6},{6,7},{7,8},{8,9},{9,10},{10,1... | collective-permute-start | bytes 3145736 | tf_op jit(solution)/shard_map/ppermute | solution.py:19
  685.1 3.0 copy-start.9
  755.6 3.5 copy-start.13
  823.9 17.5 %copy-start.1 = (f32[4,2,512,128]{3,2,1,0:T(8,128)}, f32[4,2,512,128]{3,2,1,0:T(8,128)S(1)}, u32[]{:S(2)}) copy-start(f32[4,2,512,128]{3,2,1,0:T(8,128)S(1)} %multiply_add_fusion.1) | copy-start | bytes 6291460
  824.1 16.1 %collective-permute-start.8 = (f32[4,1,512,128]{3,2,1,0:T(8,128)S(1)}, f32[4,1,512,128]{3,2,1,0:T(8,128)S(1)}, u32[]{:S(2)}, u32[]{:S(2)}) collective-permute-start(f32[4,1,512,128]{3,2,1,0:T(8,128)S(1)} %get-tuple-element.26), channel_id=1, source_target_pairs={{1,0},{2,1},{3,2},{4,3},{5,4},{6,5},{7,6},{8,7},{9,8},{10,9},{11,1... | collective-permute-start | bytes 3145736 | tf_op jit(solution)/shard_map/ppermute | solution.py:22
  826.7 14.7 %collective-permute-start.9 = (f32[4,1,512,128]{3,2,1,0:T(8,128)S(1)}, f32[4,1,512,128]{3,2,1,0:T(8,128)S(1)}, u32[]{:S(2)}, u32[]{:S(2)}) collective-permute-start(f32[4,1,512,128]{3,2,1,0:T(8,128)S(1)} %get-tuple-element.27), channel_id=1, source_target_pairs={{0,1},{1,2},{2,3},{3,4},{4,5},{5,6},{6,7},{7,8},{8,9},{9,10},{10,1... | collective-permute-start | bytes 3145736 | tf_op jit(solution)/shard_map/ppermute | solution.py:19
  972.3 3.5 copy-start.15
  975.8 2.0 copy-start.3
  977.8 17.2 %copy-start.11 = (f32[3,2,128,128]{3,2,1,0:T(8,128)S(1)}, f32[3,2,128,128]{3,2,1,0:T(8,128)}, u32[]{:S(2)}) copy-start(f32[3,2,128,128]{3,2,1,0:T(8,128)} %param.13) | copy-start | bytes 1179652
  977.8 17.3 %collective-permute-start.10 = (f32[4,1,512,128]{3,2,1,0:T(8,128)}, f32[4,1,512,128]{3,2,1,0:T(8,128)}, u32[]{:S(2)}, u32[]{:S(2)}) collective-permute-start(f32[4,1,512,128]{3,2,1,0:T(8,128)} %get-tuple-element.24), channel_id=1, source_target_pairs={{1,0},{2,1},{3,2},{4,3},{5,4},{6,5},{7,6},{8,7},{9,8},{10,9},{11,1... | collective-permute-start | bytes 3145736 | tf_op jit(solution)/shard_map/ppermute | solution.py:22
  980.5 15.1 %collective-permute-start.11 = (f32[4,1,512,128]{3,2,1,0:T(8,128)}, f32[4,1,512,128]{3,2,1,0:T(8,128)}, u32[]{:S(2)}, u32[]{:S(2)}) collective-permute-start(f32[4,1,512,128]{3,2,1,0:T(8,128)} %get-tuple-element.25), channel_id=1, source_target_pairs={{0,1},{1,2},{2,3},{3,4},{4,5},{5,6},{6,7},{7,8},{8,9},{9,10},{10,1... | collective-permute-start | bytes 3145736 | tf_op jit(solution)/shard_map/ppermute | solution.py:19
  983.5 11.4 collective-permute-start.12
  985.9 9.7 copy-start.4
  1063.4 110.6 %copy-start.14 = (pred[128]{0:T(512)(128)(4,1)S(1)}, pred[128]{0:T(512)(128)(4,1)}, u32[]{:S(2)}) copy-start(pred[128]{0:T(512)(128)(4,1)} %constant.48.clone.1) | copy-start | bytes 388
  1064.4 111.3 %copy-start.10 = (f32[3,2,128,128]{3,2,1,0:T(8,128)}, f32[3,2,128,128]{3,2,1,0:T(8,128)S(1)}, u32[]{:S(2)}) copy-start(f32[3,2,128,128]{3,2,1,0:T(8,128)S(1)} %broadcast_divide_fusion) | copy-start | bytes 1179652
  1064.5 109.5 %collective-permute-start.14 = (f32[2,1,128]{2,1,0:T(1,128)S(1)}, f32[2,1,128]{2,1,0:T(1,128)S(1)}, u32[]{:S(2)}, u32[]{:S(2)}) collective-permute-start(f32[2,1,128]{2,1,0:T(1,128)S(1)} %slice.287), channel_id=1, source_target_pairs={{0,32},{32,64},{64,96},{1,33},{33,65},{65,97},{2,34},{34,66},{66,9... | collective-permute-start | bytes 3080 | tf_op jit(solution)/shard_map/ppermute | solution.py:30
  1067.6 106.3 %collective-permute-start.13 = (f32[1,128,128]{2,1,0:T(8,128)S(1)}, f32[1,128,128]{2,1,0:T(8,128)S(1)}, u32[]{:S(2)}, u32[]{:S(2)}) collective-permute-start(f32[1,128,128]{2,1,0:T(8,128)S(1)} %get-tuple-element.42), channel_id=1, source_target_pairs={{0,1},{1,2},{2,3},{3,4},{4,5},{5,6},{6,7},{7,8},{8,9},{9,10},{10,1... | collective-permute-start | bytes 196616 | tf_op jit(solution)/shard_map/ppermute | solution.py:30
Sparse Core Ops, SparseCore 0:
  1064.4 40.3 all-reduce.12
where the time goes:
time: 1190 us; the launch traced here: 1180 us
  blocking collectives  693 us (58%)
  local copies, waits for them, and re-layouts  191 us (16%)
  other arithmetic  163 us (14%)
  waiting for transfers between devices  76.1 us (6%)
  starting transfers between devices  44.5 us (4%)
  between operations  15.5 us (1%)
    psum x6, blocking collectives, energy_of(): return lax.psum(cell_sum(residual, precon), 'space')  388 us
    psum x4, blocking collectives, precond_solve(): stride = energy / lax.psum(cell_sum(direction, applied), 'space')  238 us
    psum x1, blocking collectives, on_device(): power_sum = lax.psum(jnp.sum(own_grad * own_grad), ('lap', 'space'))  66.9 us
    scatter-add x3, other arithmetic, on_device(): jnp.zeros((constants, slab_cells), jnp.float32).at[:, src_local]  46.3 us
    scatter-add x3, other arithmetic, on_device(): jnp.zeros((constants, slab_cells), jnp.float32).at[:, rec_local].add(misfit)  46.2 us
    reduce_sum x12, other arithmetic, cell_sum(): return jnp.sum(left_field * right_field, axis=(1, 2, 3))  43.2 us
    reshape x1, local copies, waits for them, and re-layouts, on_device(): source.reshape(constants, width_x, rows_y, depth_z)  35.6 us
    reshape x1, local copies, waits for them, and re-layouts, on_device(): adjoint_source.reshape(constants, width_x, rows_y, depth_z)  35.4 us
  transfers between devices with their start and end apart: 16, of which 9 were waited for; matrix products, arithmetic and copies ran while one was open for 7% of the time, Pallas kernels for 0%

commit v1 on v0

v1 whole, which is shorter than its diff:
```python
import functools

import jax
import jax.numpy as jnp
from jax import lax
from jax.experimental import pallas as pl
from jax.experimental.pallas import tpu as pltpu
from jax.sharding import Mesh
from jax.sharding import PartitionSpec as P


HALF = 2
PLANES = 13
KEPT = 9
PAD = 8
CHUNK = 256

dual_step = 0.5
primal_step = 0.2
tv_weight = 0.5

VMEM = pl.BlockSpec(memory_space=pltpu.VMEM)
SMEM = pl.BlockSpec(memory_space=pltpu.SMEM)


def params(mib):
    return pltpu.CompilerParams(vmem_limit_bytes=mib * 2**20)


def spread_points(index, values, pieces, first, store, planes):
    points = index.shape[1]
    column = (index >> 16) * 128 + (index & 127)
    row = (index >> 7) & 511
    lanes = lax.broadcasted_iota(jnp.int32, (planes * 128, points), 0)
    right = jnp.where(lanes == column, 1.0, 0.0).astype(jnp.bfloat16)
    sub = lax.broadcasted_iota(jnp.int32, (8, points), 0)
    row = row - sub // HALF
    parts = []
    for value, count in zip(values, pieces):
        high = value.astype(jnp.bfloat16).astype(jnp.float32)
        parts.append([high, value - high][:count])
    rows = 512 * HALF
    step = 8 // HALF

    def body(k, _):
        tile = lax.broadcasted_iota(jnp.int32, (CHUNK // 8, 8, points), 0)
        mask = row[None] - step * tile == k * (CHUNK // HALF)
        for which, part in enumerate(parts):
            total = None
            for piece in part:
                left = jnp.where(mask, piece[None], 0.0).reshape(CHUNK, points).astype(jnp.bfloat16)
                got = lax.dot_general(
                    left, right, (((1,), (1,)), ((), ())), preferred_element_type=jnp.float32
                )
                total = got if total is None else total + got
            at = pl.ds(pl.multiple_of(k * CHUNK, CHUNK), CHUNK)
            for p in range(planes):
                store[which][first[which] + p, at, :] = total[:, p * 128 : (p + 1) * 128]
        return 0

    lax.fori_loop(0, rows // CHUNK, body, 0)


def scatter_kernel(core_ref, mine_ref, theirs_ref, b_ref, ob_ref, cn_ref):
    core = core_ref[0]
    points = mine_ref.shape[2]
    parity = lax.broadcasted_iota(jnp.int32, (8, points), 0) % HALF
    for slab in range(7):
        q, h = slab // 2, slab % 2
        rows = jnp.where(core == h, mine_ref[q], theirs_ref[q])
        src = rows[0:1].astype(jnp.int32)
        rec = rows[1:2].astype(jnp.int32)
        amp = jnp.where(parity == 0, rows[2:3], rows[3:4])
        obs = jnp.where(parity == 0, rows[4:5], rows[5:6])
        planes = 1 if slab == 6 else 2
        spread_points(src, [amp], [1 if slab in (0, 5, 6) else 2], [2 * slab], [b_ref], planes)
        if 1 <= slab <= 5:
            near = 1 if slab == 5 else 2
            at = 2 * slab - 2
            spread_points(
                rec, [obs, jnp.ones_like(obs)], [near, 1], [at, at], [ob_ref, cn_ref], near
            )


def neighbours(ref, t, r0):
    x = ref[t, pl.ds(PAD + r0, CHUNK), :]
    prev = ref[t, pl.ds(r0, 8), :]
    after = ref[t, pl.ds(PAD + r0 + CHUNK, 8), :]
    ext = jnp.concatenate([prev, x, after], 0)
    rows = CHUNK + 16
    down = pltpu.roll(ext, HALF, 0)[8 : 8 + CHUNK]
    up = pltpu.roll(ext, rows - HALF, 0)[8 : 8 + CHUNK]
    lane = lax.broadcasted_iota(jnp.int32, (CHUNK, 128), 1)
    low = jnp.where(lane == 0, 0.0, pltpu.roll(x, 1, 1))
    high = jnp.where(lane == 127, 0.0, pltpu.roll(x, 127, 1))
    return x, (down + up) + (low + high)


def fold(x):
    return jnp.sum(x.reshape(CHUNK // 8, 8, 128), 0)


def walk(first, last, body, carry):
    steps = 512 * HALF // CHUNK

    def step(i, c):
        t = first + i // steps
        return body(t, pl.multiple_of((i % steps) * CHUNK, CHUNK), c)

    return lax.fori_loop(0, (last - first) * steps, step, carry)


def advance(src, s_off, inv, i_off, dst, d_off, first, last, dots):
    def body(t, r0, carry):
        at = pl.ds(PAD + r0, CHUNK)
        x, q = neighbours(src, t - s_off, r0)
        q = q + (src[t - s_off - 1, at, :] + src[t - s_off + 1, at, :])
        new = inv[t - i_off, pl.ds(r0, CHUNK), :] * q
        dst[t - d_off, at, :] = new
        if not dots:
            return carry
        return carry[0] + fold(x * q), carry[1] + fold(new * q)

    zero = jnp.zeros((8, 128), jnp.float32)
    return walk(first, last, body, (zero, zero) if dots else 0)


def last_moment(src, off):
    def body(t, r0, carry):
        x, q = neighbours(src, t - off, r0)
        q = q + 2.0 * src[t - off + 1, pl.ds(PAD + r0, CHUNK), :]
        return carry + fold(x * q)

    return walk(4, 8, body, jnp.zeros((8, 128), jnp.float32))


def clear_pads(*refs):
    for ref in refs:
        zero = jnp.zeros((8, 128), jnp.float32)
        for t in range(ref.shape[0]):
            ref[t, 0:PAD, :] = zero
            ref[t, ref.shape[1] - PAD :, :] = zero


def message(moments):
    sub = lax.broadcasted_iota(jnp.int32, (8, 128), 0)
    lane = lax.broadcasted_iota(jnp.int32, (8, 128), 1)
    out = jnp.zeros((8, 128), jnp.float32)
    for k, moment in enumerate(moments):
        for c in range(HALF):
            total = jnp.sum(jnp.where(sub % HALF == c, moment, 0.0))
            out = out + jnp.where((sub == k) & (lane == c), total, 0.0)
    return out


def coefficients(moments):
    m = [moments[k : k + 1, :] for k in range(6)]

    def product(p, shift):
        total = 0.0
        for i, a in enumerate(p):
            for j, b in enumerate(p):
                total = total + a * b * (m[i + j] - m[i + j + 1] if shift else m[i + j])
        return total

    one = jnp.ones_like(m[0])
    z, p, energy = [one], [one], m[0]
    x = [0.0 * one] * 3
    for it in range(3):
        stride = energy / product(p, True)
        x = [x[i] + (stride * p[i] if i < len(p) else 0.0) for i in range(3)]
        if it < 2:
            applied = [a - b for a, b in zip(p + [0.0 * one], [0.0 * one] + p)]
            z = [a - stride * b for a, b in zip(z + [0.0 * one], applied)]
            new = product(z, False)
            p = [a + new / energy * b for a, b in zip(z, p + [0.0 * one])]
            energy = new
    lane = lax.broadcasted_iota(jnp.int32, (1, 128), 1)
    sub = lax.broadcasted_iota(jnp.int32, (8, 128), 0)
    out = []
    for v in x:
        value = [jnp.sum(jnp.where(lane == c, v, 0.0)) for c in range(HALF)]
        out.append(jnp.where(sub % HALF == 0, value[0], value[1]))
    return out


def times(pattern, x):
    return (pattern[None] * x.reshape(CHUNK // 8, 8, 128)).reshape(CHUNK, 128)


def forward_kernel(par, own_m, own_t, near_m, near_t, b, inv, v0, v1, v2, msg):
    core = par[5]
    slabs = (
        (near_m, near_t, 0, 0, 2), (near_m, near_t, 0, 1, 2),
        (own_m, own_t, 0, 0, None), (own_m, own_t, 0, 1, None),
        (near_m, near_t, 2, 0, 3), (near_m, near_t, 2, 1, 3), (near_m, near_t, 4, 0, 4),
    )
    clear_pads(v0, v1, v2)
    for slab, (mine, theirs, base, h, flag) in enumerate(slabs):
        valid = 1.0 if flag is None else par[flag]
        planes = 1 if slab == 6 else 2

        def fill(p, _, mine=mine, theirs=theirs, base=base, h=h, valid=valid, slab=slab):
            sigma = jnp.where(core == float(h), mine[base + p], theirs[base + p])
            for c in range(HALF):
                inv[2 * slab + p, pl.ds(c, 512, stride=HALF), :] = valid / (6.0 + par[c] * sigma)
            return 0

        lax.fori_loop(0, planes, fill, 0)

    def start(dots):
        def body(t, r0, carry):
            right = b[t, pl.ds(r0, CHUNK), :]
            new = inv[t, pl.ds(r0, CHUNK), :] * right
            v0[t, pl.ds(PAD + r0, CHUNK), :] = new
            return carry + fold(new * right) if dots else carry

        return body

    zero = jnp.zeros((8, 128), jnp.float32)
    walk(0, 4, start(False), 0)
    m0 = walk(4, 8, start(True), zero)
    walk(8, 13, start(False), 0)
    advance(v0, 0, inv, 0, v1, 1, 1, 4, False)
    m1, m2 = advance(v0, 0, inv, 0, v1, 1, 4, 8, True)
    advance(v0, 0, inv, 0, v1, 1, 8, 12, False)
    advance(v1, 1, inv, 0, v2, 2, 2, 4, False)
    m3, m4 = advance(v1, 1, inv, 0, v2, 2, 4, 8, True)
    advance(v1, 1, inv, 0, v2, 2, 8, 11, False)
    m5 = last_moment(v2, 2)
    msg[...] = message([m0, m1, m2, m3, m4, m5])


def adjoint_kernel(total, inv, v0, v1, v2, ob, cn, wave, u0, u1, u2, msg):
    a = coefficients(total[...])
    clear_pads(u0, u1, u2)

    def start(own):
        def body(t, r0, carry):
            at = pl.ds(PAD + r0, CHUNK)
            here = pl.ds(r0, CHUNK)
            w = times(a[0], v0[t, at, :]) + times(a[1], v1[t - 1, at, :])
            w = w + times(a[2], v2[t - 2, at, :])
            right = cn[t - 2, here, :] * w - ob[t - 2, here, :]
            new = inv[t, here, :] * right
            u0[t - 2, at, :] = new
            if not own:
                return carry
            wave[t - 4, here, :] = w
            return carry + fold(new * right)

        return body

    zero = jnp.zeros((8, 128), jnp.float32)
    walk(2, 4, start(False), 0)
    m0 = walk(4, 8, start(True), zero)
    walk(8, 11, start(False), 0)
    advance(u0, 2, inv, 0, u1, 3, 3, 4, False)
    m1, m2 = advance(u0, 2, inv, 0, u1, 3, 4, 8, True)
    advance(u0, 2, inv, 0, u1, 3, 8, 10, False)
    m3, m4 = advance(u1, 3, inv, 0, u2, 4, 4, 8, True)
    advance(u1, 3, inv, 0, u2, 4, 8, 9, False)
    m5 = last_moment(u2, 4)
    msg[...] = message([m0, m1, m2, m3, m4, m5])


def gradient_kernel(par, total, wave, u0, u1, u2, out, held):
    a = coefficients(total[...])
    sub = lax.broadcasted_iota(jnp.int32, (8, 128), 0)
    square = jnp.where(sub % HALF == 0, par[0], par[1])
    a = [-square * v for v in a]

    def body(t, r0, carry):
        at = pl.ds(PAD + r0, CHUNK)
        x = times(a[0], u0[t - 2, at, :]) + times(a[1], u1[t - 3, at, :])
        x = x + times(a[2], u2[t - 4, at, :])
        held[pl.ds((t - 4) * 1024 + r0, CHUNK), :] = x * wave[t - 4, pl.ds(r0, CHUNK), :]
        return carry

    walk(4, 8, body, 0)
    for t in range(4):
        for band in range(4):
            at = t * 1024 + band * 256
            both = held[pl.ds(at, 128, stride=HALF), :] + held[pl.ds(at + 1, 128, stride=HALF), :]
            out[band * 2 + t // 2, t % 2] = both


def power_kernel(parts, own, msg):
    g = parts[0]
    for k in range(1, 8):
        g = g + parts[k]
    own[...] = g
    msg[...] = jnp.full((128, 128), jnp.sum(g * g), jnp.float32)


def struct(*shape):
    return jax.ShapeDtypeStruct(shape, jnp.float32)


def moved(x, axis, by):
    peers = lax.axis_size(axis)
    return lax.ppermute(x, axis, [(i, i + by) for i in range(peers) if 0 <= i + by < peers])


def swapped(x):
    return lax.ppermute(x, "core", [(0, 1), (1, 0)])


def pair_sum(x):
    for masks in ((1, 2, 3), (4, 8, 12)):
        x = x + sum(lax.ppermute(x, "pair", [(i, i ^ d) for i in range(16)]) for d in masks)
    return x


def on_device(slowness, damping, src_index, src_amp, rec_index, observed, dual):
    width_x, rows_y, depth_z = slowness.shape
    slab_cells = width_x * rows_y * depth_z
    lap, pair, core = (lax.axis_index(name) for name in ("lap", "pair", "core"))
    pairs = lax.axis_size("pair")
    offset = (pair * 2 + core) * slab_cells

    squared = damping * damping
    own_sq = lax.dynamic_slice_in_dim(squared, core * HALF, HALF)
    flags = jnp.stack([pair >= 1, pair + 1 < pairs, pair + 2 < pairs, core == 1])
    par = jnp.concatenate([own_sq, flags.astype(jnp.float32), jnp.zeros(2, jnp.float32)])
    core_in = core.astype(jnp.int32).reshape(1)

    index = jnp.stack([src_index - offset, rec_index - offset]).astype(jnp.float32)
    blank = jnp.zeros_like(index)
    lists = jnp.stack(
        [jnp.concatenate([index, src_amp[2 * k : 2 * k + 2], observed[2 * k : 2 * k + 2], blank])
         for k in range(2)]
    )
    around = [moved(lists, "pair", 1), lists, moved(lists, "pair", -1), moved(lists, "pair", -2)]
    stack = jnp.stack(around)
    mine = lax.dynamic_index_in_dim(stack, core, 1, False)
    theirs = swapped(lax.dynamic_index_in_dim(stack, 1 - core, 1, False))

    own_t = swapped(slowness)
    near_m = jnp.concatenate(
        [moved(slowness, "pair", 1), moved(slowness, "pair", -1), moved(slowness[:1], "pair", -2)]
    )
    near_t = swapped(near_m)

    b, ob, cn = pl.pallas_call(
        scatter_kernel,
        out_shape=(struct(PLANES, 1024, 128), struct(KEPT, 1024, 128), struct(KEPT, 1024, 128)),
        in_specs=[SMEM, VMEM, VMEM],
        out_specs=(VMEM,) * 3,
        compiler_params=params(24),
        name="scatter",
    )(core_in, mine, theirs)

    padded = 1024 + 2 * PAD
    inv, v0, v1, v2, msg = pl.pallas_call(
        forward_kernel,
        out_shape=(
            struct(PLANES, 1024, 128), struct(13, padded, 128), struct(11, padded, 128),
            struct(9, padded, 128), struct(8, 128),
        ),
        in_specs=[SMEM] + [VMEM] * 5,
        out_specs=(VMEM,) * 5,
        compiler_params=params(40),
        name="forward",
    )(par, slowness, own_t, near_m, near_t, b)

    wave, u0, u1, u2, msg = pl.pallas_call(
        adjoint_kernel,
        out_shape=(
            struct(4, 1024, 128), struct(9, padded, 128), struct(7, padded, 128),
            struct(5, padded, 128), struct(8, 128),
        ),
        in_specs=[VMEM] * 7,
        out_specs=(VMEM,) * 5,
        compiler_params=params(50),
        name="adjoint",
    )(pair_sum(msg), inv, v0, v1, v2, ob, cn)

    parts = pl.pallas_call(
        gradient_kernel,
        out_shape=struct(8, 2, 128, 128),
        in_specs=[SMEM] + [VMEM] * 5,
        out_specs=VMEM,
        scratch_shapes=[pltpu.VMEM((4096, 128), jnp.float32)],
        compiler_params=params(24),
        name="gradient",
    )(par, pair_sum(msg), wave, u0, u1, u2)

    parts = lax.all_to_all(parts, ("lap", "core"), 0, 0, tiled=True)
    own_grad, power = pl.pallas_call(
        power_kernel,
        out_shape=(struct(2, 128, 128), struct(128, 128)),
        in_specs=[VMEM],
        out_specs=(VMEM, VMEM),
        name="power",
    )(parts)
    power = lax.all_to_all(power, ("lap", "pair", "core"), 0, 0, tiled=True)
    power_sum = jnp.sum(power[:, 0])

    band_rows = rows_y // lax.axis_size("lap")
    start_y = lap * band_rows
    space_pos = pair * 2 + core
    slabs = pairs * 2
    total_cells = slab_cells * slabs
    scaled = own_grad / jnp.sqrt(power_sum / total_cells + 1e-06)
    padded_model = jnp.pad(slowness, ((0, 0), (0, 1), (0, 0)))
    window = lax.dynamic_slice_in_dim(padded_model, start_y, band_rows + 1, 1)
    own_model = window[:, :band_rows]
    x_glob = space_pos * width_x + jnp.arange(width_x, dtype=jnp.int32)
    last_x = (x_glob == width_x * slabs - 1)[:, None, None]
    y_glob = start_y + jnp.arange(band_rows, dtype=jnp.int32)
    last_y = (y_glob == rows_y - 1)[None, :, None]
    following = lax.dynamic_slice_in_dim(
        jnp.where(core == 0, own_t[:1], near_t[2:3]), start_y, band_rows, 1
    )
    step_x = jnp.where(last_x, 0.0, jnp.concatenate([own_model[1:], following], 0) - own_model)
    step_y = jnp.where(last_y, 0.0, window[:, 1:] - own_model)
    step_z = jnp.concatenate(
        [own_model[:, :, 1:] - own_model[:, :, :-1], jnp.zeros_like(own_model[:, :, :1])], 2
    )
    dual_trial = dual + dual_step * jnp.stack([step_x, step_y, step_z])
    magnitude = jnp.sqrt(jnp.sum(dual_trial * dual_trial, axis=0))
    dual_next = dual_trial / jnp.maximum(1.0, magnitude / tv_weight)
    comp_x = jnp.where(last_x, 0.0, dual_next[0])
    comp_y = jnp.where(last_y, 0.0, dual_next[1])
    comp_z = jnp.concatenate([dual_next[2][:, :, :-1], jnp.zeros_like(dual_next[2][:, :, :1])], 2)
    prior_x = moved(comp_x[-1:], ("pair", "core"), 1)
    back_x = jnp.concatenate([prior_x, comp_x[:-1]], 0) - comp_x
    prior_y = moved(comp_y[:, -1:], "lap", 1)
    back_y = jnp.concatenate([prior_y, comp_y[:, :-1]], 1) - comp_y
    back_z = jnp.concatenate([jnp.zeros_like(comp_z[:, :, :1]), comp_z[:, :, :-1]], 2) - comp_z
    model = own_model - primal_step * (scaled + back_x + back_y + back_z)
    return (model, dual_next)


def solution(mesh):
    space = mesh.devices.shape[1]
    mesh = Mesh(mesh.devices.reshape(-1, space // 2, 2), ("lap", "pair", "core"))
    both = ("pair", "core")
    in_specs = (
        P(both, None, None),
        P("lap"),
        P(both),
        P("lap", both),
        P(both),
        P("lap", both),
        P(None, both, "lap", None),
    )
    out_specs = (P(both, "lap", None), P(None, both, "lap", None))
    return jax.shard_map(
        on_device, mesh=mesh, in_specs=in_specs, out_specs=out_specs, check_vma=False
    )
```

time: 1190 us -> 219 us (0.18)
  blocking collectives: 693 us -> 0 us
  local copies, waits for them, and re-layouts: 191 us -> 23.1 us
  other arithmetic: 163 us -> 5.23 us
  Pallas kernels: 0 us -> 81.7 us
  waiting for transfers between devices: 76.1 us -> 48.5 us
  starting transfers between devices: 44.5 us -> 58.4 us
  between operations: 15.5 us -> 1.64 us
    psum x11 -> x0, blocking collectives: 693 us -> none  [the longest x6 388 us: energy_of(): return lax.psum(cell_sum(residual, precon), 'space')]
    scatter-add x6 -> x0, other arithmetic: 92.5 us -> none  [the longest x3 46.3 us: on_device(): jnp.zeros((constants, slab_cells), jnp.float32).at[:, src_local]]
    pallas_call x0 -> x5, Pallas kernels: none -> 81.7 us  [the longest x1 27 us: on_device(): pl.pallas_call(adjoint_kernel, out_shape=(struct(4, 1024, 128), struct(9,...]
    reshape x2 -> x0, local copies, waits for them, and re-layouts: 70.9 us -> none  [the longest x1 35.6 us: on_device(): source.reshape(constants, width_x, rows_y, depth_z)]
    scatter-add x4 -> x0, local copies, waits for them, and re-layouts: 69.1 us -> none  [the longest x2 34.5 us: on_device(): jnp.zeros((constants, slab_cells), jnp.float32).at[:, src_local]]
    reduce_sum x14 -> x1, other arithmetic: 48.6 us -> 0.68 us  [on_device(): power_sum = jnp.sum(power[:, 0])]
    psum x1 -> x0, waiting for transfers between devices: 35.1 us -> none  [on_device(): summed = lax.psum(partial_grad, 'lap')]
    add x1 -> x0, local copies, waits for them, and re-layouts: 31.2 us -> none  [precond_solve(): iterate = iterate + spread(stride) * direction]
  transfers between devices with their start and end apart: 16 -> 25, of which waited for: 9 -> 13; matrix products, arithmetic and copies ran while one was open for 7% -> 4% of each run, Pallas kernels for 0% -> 12%
where the time goes in v1:
time: 219 us
  Pallas kernels  81.7 us (37%)
  starting transfers between devices  58.4 us (27%)
  waiting for transfers between devices  48.5 us (22%)
  local copies, waits for them, and re-layouts  23.1 us (11%)
  other arithmetic  5.23 us (2%)
    pallas_call x1, Pallas kernels, on_device(): pl.pallas_call(adjoint_kernel, out_shape=(struct(4, 1024, 128), struct(9,...  27 us
    pallas_call x1, Pallas kernels, on_device(): pl.pallas_call(forward_kernel, out_shape=(struct(PLANES, 1024, 128), stru...  25.2 us
    pallas_call x1, Pallas kernels, on_device(): pl.pallas_call(scatter_kernel, out_shape=(struct(PLANES, 1024, 128), stru...  24.8 us
    ppermute x8, starting transfers between devices, moved(): lax.ppermute(x, axis, [(i, i + by) for i in range(peers) if 0 <= i + by <...  21.6 us
    ppermute x8, waiting for transfers between devices, moved(): lax.ppermute(x, axis, [(i, i + by) for i in range(peers) if 0 <= i + by <...  21.6 us
    unnamed x34, local copies, waits for them, and re-layouts  18.8 us
    ppermute x12, starting transfers between devices, pair_sum(): lax.ppermute(x, 'pair', [(i, i ^ d) for i in range(16)])  17.1 us
    all_to_all x1, waiting for transfers between devices, on_device(): parts = lax.all_to_all(parts, ('lap', 'core'), 0, 0, tiled=True)  11.5 us
  transfers between devices with their start and end apart: 25, of which 13 were waited for; matrix products, arithmetic and copies ran while one was open for 4% of the time, Pallas kernels for 12%

profile of v1, /device:TPU:1, one launch (start us, length us, event | category | flops | bytes accessed | tf_op | source)
XLA Modules:
  0.0 218.6 jit_solution(5941823879151148148)
XLA Ops:
  0.7 4.5 %collective-permute-start.1 = (f32[2,512,128]{2,1,0:T(8,128)}, f32[2,512,128]{2,1,0:T(8,128)S(1)}, u32[]{:S(2)}, u32[]{:S(2)}) collective-permute-start(f32[2,512,128]{2,1,0:T(8,128)} %own_m.1), channel_id=1, source_target_pairs={{0,2},{2,4},{4,6},{6,8},{8,10},{10,12},{12,14},{14,16},{16,18},{18... | collective-permute-start | bytes 1572872 | tf_op jit(solution)/shard_map/ppermute | solution.py:302
  5.2 1.3 collective-permute-start.2
  6.5 1.0 slice.68
  7.5 1.3 collective-permute-start.3
  8.8 0.7 broadcast_subtract_fusion
  9.6 0.7 mul.35
  10.4 5.6 %collective-permute-done.1 = f32[2,512,128]{2,1,0:T(8,128)S(1)} collective-permute-done((f32[2,512,128]{2,1,0:T(8,128)}, f32[2,512,128]{2,1,0:T(8,128)S(1)}, u32[]{:S(2)}, u32[]{:S(2)}) %collective-permute-start.1) | collective-permute-done | bytes 524320 | tf_op jit(solution)/shard_map/ppermute | solution.py:302
  16.1 9.5 %collective-permute-done.2 = f32[2,512,128]{2,1,0:T(8,128)S(1)} collective-permute-done((f32[2,512,128]{2,1,0:T(8,128)}, f32[2,512,128]{2,1,0:T(8,128)S(1)}, u32[]{:S(2)}, u32[]{:S(2)}) %collective-permute-start.2) | collective-permute-done | bytes 524320 | tf_op jit(solution)/shard_map/ppermute | solution.py:302
  25.7 1.9 collective-permute-start.4
  27.8 1.3 collective-permute-start.6
  29.1 1.3 collective-permute-start.7
  30.4 5.0 %collective-permute-start.5 = (f32[2,8,1024]{2,1,0:T(8,128)S(1)}, f32[2,8,1024]{2,1,0:T(8,128)S(1)}, u32[]{:S(2)}, u32[]{:S(2)}) collective-permute-start(f32[2,8,1024]{2,1,0:T(8,128)S(1)} %get-tuple-element.41), channel_id=1, source_target_pairs={{0,2},{2,4},{4,6},{6,8},{8,10},{10,12},{12,14},{14,16},{16,18},{18... | collective-permute-start | bytes 196616 | tf_op jit(solution)/shard_map/ppermute | solution.py:302
  35.8 0.8 fusion.1
  37.2 6.5 %collective-permute-done.7 = f32[2,8,1024]{2,1,0:T(8,128)S(1)} collective-permute-done((f32[2,8,1024]{2,1,0:T(8,128)S(1)}, f32[2,8,1024]{2,1,0:T(8,128)S(1)}, u32[]{:S(2)}, u32[]{:S(2)}) %collective-permute-start.7) | collective-permute-done | bytes 65568 | tf_op jit(solution)/shard_map/ppermute | solution.py:302
  43.6 0.7 dynamic-slice_bitcast_fusion
  44.9 0.9 pad_bitcast_fusion
  46.1 24.8 %scatter.1 = (f32[13,1024,128]{2,1,0:T(8,128)S(1)}, f32[9,1024,128]{2,1,0:T(8,128)S(1)}, f32[9,1024,128]{2,1,0:T(8,128)S(1)}) custom-call(s32[1]{0:T(128)} %bitcast.4.core_ref, f32[4,8,1024]{2,1,0:T(8,128)S(1)} %get-tuple-element.37.mine_ref, f32[4,8,1024]{2,1,0:T(8,128)S(1)} %collective-permute-done.8.theirs_ref), custom_call_target="tpu_custom_call" | custom-call | tf_op jit(solution)/shard_map/scatter/pallas_call | solution.py:345
  71.0 2.7 %copy-done.1 = f32[13,1024,128]{2,1,0:T(8,128)} copy-done((f32[13,1024,128]{2,1,0:T(8,128)}, f32[13,1024,128]{2,1,0:T(8,128)S(1)}, u32[]{:S(2)}) %copy-start.1) | copy-done | bytes 6815768
  73.7 2.1 copy-done.5
  75.8 2.2 copy-done.6
  77.9 25.2 %forward.1 = (f32[13,1024,128]{2,1,0:T(8,128)}, f32[13,1040,128]{2,1,0:T(8,128)}, f32[11,1040,128]{2,1,0:T(8,128)S(1)}, f32[9,1040,128]{2,1,0:T(8,128)S(1)}, f32[8,128]{1,0:T(8,128)S(1)}) custom-call(f32[8]{0:T(128)S(1)} %get-tuple-element.49.par, f32[2,512,128]{2,1,0:T(8,128)S(1)} %copy-done, f32[2,512,128]{2,1,0:T(8,128)} %collective-permute-done.own_t, ...), custom_call_target="tpu_custom_call" | custom-call | tf_op jit(solution)/shard_map/forward/pallas_call | solution.py:355
  103.1 2.4 %copy-done.2 = f32[11,1040,128]{2,1,0:T(8,128)} copy-done((f32[11,1040,128]{2,1,0:T(8,128)}, f32[11,1040,128]{2,1,0:T(8,128)S(1)}, u32[]{:S(2)}) %copy-start.2) | copy-done | bytes 5857304
  105.5 2.1 copy-done.3
  107.7 4.9 %collective-permute-start.11 = (f32[8,128]{1,0:T(8,128)S(1)}, f32[8,128]{1,0:T(8,128)S(1)}, u32[]{:S(2)}, u32[]{:S(2)}) collective-permute-start(f32[8,128]{1,0:T(8,128)S(1)} %get-tuple-element.18), channel_id=1, source_target_pairs={{0,6},{2,4},{4,2},{6,0},{8,14},{10,12},{12,10},{14,8},{16,22},{18,... | collective-permute-start | bytes 12296 | tf_op jit(solution)/shard_map/ppermute | solution.py:311
  113.2 1.0 slice.89
  114.2 2.4 %collective-permute-done.10 = f32[8,128]{1,0:T(8,128)S(1)} collective-permute-done((f32[8,128]{1,0:T(8,128)S(1)}, f32[8,128]{1,0:T(8,128)S(1)}, u32[]{:S(2)}, u32[]{:S(2)}) %collective-permute-start.10) | collective-permute-done | bytes 4128 | tf_op jit(solution)/shard_map/ppermute | solution.py:311
  116.6 4.4 %collective-permute-start.14 = (f32[8,128]{1,0:T(8,128)S(1)}, f32[8,128]{1,0:T(8,128)S(1)}, u32[]{:S(2)}, u32[]{:S(2)}) collective-permute-start(f32[8,128]{1,0:T(8,128)S(1)} %add_add_fusion.3), channel_id=1, source_target_pairs={{0,24},{2,26},{4,28},{6,30},{8,16},{10,18},{12,20},{14,22},{16,8},... | collective-permute-start | bytes 12296 | tf_op jit(solution)/shard_map/ppermute | solution.py:311
  122.0 3.0 %collective-permute-done.13 = f32[8,128]{1,0:T(8,128)S(1)} collective-permute-done((f32[8,128]{1,0:T(8,128)S(1)}, f32[8,128]{1,0:T(8,128)S(1)}, u32[]{:S(2)}, u32[]{:S(2)}) %collective-permute-start.13) | collective-permute-done | bytes 4128 | tf_op jit(solution)/shard_map/ppermute | solution.py:311
  125.0 27.0 %adjoint.1 = (f32[4,1024,128]{2,1,0:T(8,128)S(1)}, f32[9,1040,128]{2,1,0:T(8,128)}, f32[7,1040,128]{2,1,0:T(8,128)}, f32[5,1040,128]{2,1,0:T(8,128)}, f32[8,128]{1,0:T(8,128)S(1)}) custom-call(f32[8,128]{1,0:T(8,128)S(1)} %add_add_fusion.2.total, f32[13,1024,128]{2,1,0:T(8,128)} %get-tuple-element.19.inv, f32[13,1040,128]{2,1,0:T(8,128)} %get-tuple-element.20.v0, ...), custom_call_target="tpu_custom_call" | custom-call | tf_op jit(solution)/shard_map/adjoint/pallas_call | solution.py:367
  152.0 2.1 collective-permute-start.17
  154.1 0.8 collective-permute-start.16
  155.6 2.4 %collective-permute-done.16 = f32[8,128]{1,0:T(8,128)S(1)} collective-permute-done((f32[8,128]{1,0:T(8,128)S(1)}, f32[8,128]{1,0:T(8,128)S(1)}, u32[]{:S(2)}, u32[]{:S(2)}) %collective-permute-start.16) | collective-permute-done | bytes 4128 | tf_op jit(solution)/shard_map/ppermute | solution.py:311
  158.5 1.2 collective-permute-start.19
  159.7 1.7 collective-permute-start.18
  162.4 2.4 %copy-done.4 = f32[9,1040,128]{2,1,0:T(8,128)S(1)} copy-done((f32[9,1040,128]{2,1,0:T(8,128)S(1)}, f32[9,1040,128]{2,1,0:T(8,128)}, u32[]{:S(2)}) %copy-start.4) | copy-done | bytes 4792344
  164.8 2.1 copy-done.7
  166.9 1.7 copy-done.8
  168.6 2.6 %gradient.1 = f32[8,2,128,128]{3,2,1,0:T(8,128)} custom-call(f32[8]{0:T(128)S(1)} %get-tuple-element.49.par, f32[8,128]{1,0:T(8,128)S(1)} %add_add_fusion.total, f32[4,1024,128]{2,1,0:T(8,128)S(1)} %get-tuple-element.26.wave, f32[9,1040,128]{2,1,0:T(8,128)S(1)} %copy-done.4, f32[7,1040,128]{2,1,0:T(8,128)S(1)} %copy-done.7, f32[5,1040,128]{2,1,0:T(8,128)S(1)} %copy-done.8), custom_call_target="tpu_custom_call" | custom-call | tf_op jit(solution)/shard_map/gradient/pallas_call | solution.py:379
  171.3 10.5 %all-to-all-start = ((f32[8,2,128,128]{3,2,1,0:T(8,128)}), f32[8,2,128,128]{3,2,1,0:T(8,128)S(1)}, u32[]{:S(2)}, u32[]{:S(2)}) async-start(f32[8,2,128,128]{3,2,1,0:T(8,128)} %gradient.1), calls=%async_computation | async-start | bytes 2097152 | tf_op jit(solution)/shard_map/all_to_all | solution.py:389
  182.0 3.3 %collective-permute-start.22 = (f32[2,1,128]{2,1,0:T(1,128)S(1)}, f32[2,1,128]{2,1,0:T(1,128)S(1)}, u32[]{:S(2)}, u32[]{:S(2)}) collective-permute-start(f32[2,1,128]{2,1,0:T(1,128)S(1)} %slice.95), channel_id=1, source_target_pairs={{0,32},{32,64},{64,96},{1,33},{33,65},{65,97},{2,34},{34,66},{66,9... | collective-permute-start | bytes 3080 | tf_op jit(solution)/shard_map/ppermute | solution.py:302
  185.3 11.5 %all-to-all-done.parts = f32[8,2,128,128]{3,2,1,0:T(8,128)S(1)} async-done(((f32[8,2,128,128]{3,2,1,0:T(8,128)}), f32[8,2,128,128]{3,2,1,0:T(8,128)S(1)}, u32[]{:S(2)}, u32[]{:S(2)}) %all-to-all-start) | async-done | bytes 1048608 | tf_op jit(solution)/shard_map/all_to_all | solution.py:389
  196.9 1.0 copy-done.9
  197.9 2.1 power.1
  199.9 6.2 %all-to-all-start.1 = ((f32[128,1,128]{2,1,0:T(1,128)}), f32[128,1,128]{2,1,0:T(1,128)S(1)}, u32[]{:S(2)}, u32[]{:S(2)}) async-start(f32[128,1,128]{2,1,0:T(1,128)} %bitcast.47), calls=%async_computation.1 | async-start | bytes 131072 | tf_op jit(solution)/shard_map/all_to_all | solution.py:397
  206.2 3.7 %collective-permute-start.21 = (f32[1,128,128]{2,1,0:T(8,128)S(1)}, f32[1,128,128]{2,1,0:T(8,128)S(1)}, u32[]{:S(2)}, u32[]{:S(2)}) collective-permute-start(f32[1,128,128]{2,1,0:T(8,128)S(1)} %get-tuple-element.38), channel_id=1, source_target_pairs={{0,1},{1,2},{2,3},{3,4},{4,5},{5,6},{6,7},{7,8},{8,9},{9,10},{10,1... | collective-permute-start | bytes 196616 | tf_op jit(solution)/shard_map/ppermute | solution.py:302
  209.8 5.7 %all-to-all-done.1 = f32[128,1,128]{2,1,0:T(1,128)S(1)} async-done(((f32[128,1,128]{2,1,0:T(1,128)}), f32[128,1,128]{2,1,0:T(1,128)S(1)}, u32[]{:S(2)}, u32[]{:S(2)}) %all-to-all-start.1) | async-done | bytes 65568 | tf_op jit(solution)/shard_map/all_to_all | solution.py:397
  215.5 0.7 slice_reduce_fusion
  216.9 1.7 fusion.13
  (77 shorter events, 6.4 us)
Async XLA Ops:
  0.6 34.7 %copy-start = (f32[2,512,128]{2,1,0:T(8,128)S(1)}, f32[2,512,128]{2,1,0:T(8,128)}, u32[]{:S(2)}) copy-start(f32[2,512,128]{2,1,0:T(8,128)} %own_m.1) | copy-start | bytes 1572868
  0.6 27.0 %copy-start.14 = (f32[4,1024]{1,0:T(4,128)S(1)}, f32[4,1024]{1,0:T(4,128)}, u32[]{:S(2)}) copy-start(f32[4,1024]{1,0:T(4,128)} %param.12) | copy-start | bytes 49156
  0.6 27.0 %copy-start.13 = (f32[4,1024]{1,0:T(4,128)S(1)}, f32[4,1024]{1,0:T(4,128)}, u32[]{:S(2)}) copy-start(f32[4,1024]{1,0:T(4,128)} %param.10) | copy-start | bytes 49156
  0.7 15.4 %collective-permute-start.1 = (f32[2,512,128]{2,1,0:T(8,128)}, f32[2,512,128]{2,1,0:T(8,128)S(1)}, u32[]{:S(2)}, u32[]{:S(2)}) collective-permute-start(f32[2,512,128]{2,1,0:T(8,128)} %own_m.1), channel_id=1, source_target_pairs={{0,2},{2,4},{4,6},{6,8},{8,10},{10,12},{12,14},{14,16},{16,18},{18... | collective-permute-start | bytes 1572872 | tf_op jit(solution)/shard_map/ppermute | solution.py:302
  5.2 20.4 %collective-permute-start.2 = (f32[2,512,128]{2,1,0:T(8,128)}, f32[2,512,128]{2,1,0:T(8,128)S(1)}, u32[]{:S(2)}, u32[]{:S(2)}) collective-permute-start(f32[2,512,128]{2,1,0:T(8,128)} %own_m.1), channel_id=1, source_target_pairs={{2,0},{4,2},{6,4},{8,6},{10,8},{12,10},{14,12},{16,14},{18,16},{20... | collective-permute-start | bytes 1572872 | tf_op jit(solution)/shard_map/ppermute | solution.py:302
  7.5 18.2 %collective-permute-start.3 = (f32[1,512,128]{2,1,0:T(8,128)S(1)}, f32[1,512,128]{2,1,0:T(8,128)S(1)}, u32[]{:S(2)}, u32[]{:S(2)}) collective-permute-start(f32[1,512,128]{2,1,0:T(8,128)S(1)} %slice.68), channel_id=1, source_target_pairs={{4,0},{6,2},{8,4},{10,6},{12,8},{14,10},{16,12},{18,14},{20,16},{2... | collective-permute-start | bytes 786440 | tf_op jit(solution)/shard_map/ppermute | solution.py:302
  25.7 52.2 %collective-permute-start.4 = (f32[5,512,128]{2,1,0:T(8,128)S(1)}, f32[5,512,128]{2,1,0:T(8,128)S(1)}, u32[]{:S(2)}, u32[]{:S(2)}) collective-permute-start(f32[5,512,128]{2,1,0:T(8,128)S(1)} %constant_dynamic-update-slice_fusion.near_m), channel_id=1, source_target_pairs={{0,1},{1,0},{2,3},{3,2},{4,5},{5,4},{6,7},{7,6},{8,9},{9,8},{10,11... | collective-permute-start | bytes 3932168 | tf_op jit(solution)/shard_map/ppermute | solution.py:306
  27.8 9.4 %collective-permute-start.6 = (f32[2,8,1024]{2,1,0:T(8,128)S(1)}, f32[2,8,1024]{2,1,0:T(8,128)S(1)}, u32[]{:S(2)}, u32[]{:S(2)}) collective-permute-start(f32[2,8,1024]{2,1,0:T(8,128)S(1)} %get-tuple-element.41), channel_id=1, source_target_pairs={{2,0},{4,2},{6,4},{8,6},{10,8},{12,10},{14,12},{16,14},{18,16},{20... | collective-permute-start | bytes 196616 | tf_op jit(solution)/shard_map/ppermute | solution.py:302
  29.1 14.6 %collective-permute-start.7 = (f32[2,8,1024]{2,1,0:T(8,128)S(1)}, f32[2,8,1024]{2,1,0:T(8,128)S(1)}, u32[]{:S(2)}, u32[]{:S(2)}) collective-permute-start(f32[2,8,1024]{2,1,0:T(8,128)S(1)} %get-tuple-element.41), channel_id=1, source_target_pairs={{4,0},{6,2},{8,4},{10,6},{12,8},{14,10},{16,12},{18,14},{20,16},{2... | collective-permute-start | bytes 196616 | tf_op jit(solution)/shard_map/ppermute | solution.py:302
  30.4 13.3 %collective-permute-start.5 = (f32[2,8,1024]{2,1,0:T(8,128)S(1)}, f32[2,8,1024]{2,1,0:T(8,128)S(1)}, u32[]{:S(2)}, u32[]{:S(2)}) collective-permute-start(f32[2,8,1024]{2,1,0:T(8,128)S(1)} %get-tuple-element.41), channel_id=1, source_target_pairs={{0,2},{2,4},{4,6},{6,8},{8,10},{10,12},{12,14},{14,16},{16,18},{18... | collective-permute-start | bytes 196616 | tf_op jit(solution)/shard_map/ppermute | solution.py:302
  35.4 42.5 %collective-permute-start = (f32[2,512,128]{2,1,0:T(8,128)S(1)}, f32[2,512,128]{2,1,0:T(8,128)}, u32[]{:S(2)}, u32[]{:S(2)}) collective-permute-start(f32[2,512,128]{2,1,0:T(8,128)S(1)} %copy-done), channel_id=1, source_target_pairs={{0,1},{1,0},{2,3},{3,2},{4,5},{5,4},{6,7},{7,6},{8,9},{9,8},{10,11... | collective-permute-start | bytes 1572872 | tf_op jit(solution)/shard_map/ppermute | solution.py:306
  44.3 1.8 collective-permute-start.8
  71.0 2.7 %copy-start.1 = (f32[13,1024,128]{2,1,0:T(8,128)}, f32[13,1024,128]{2,1,0:T(8,128)S(1)}, u32[]{:S(2)}) copy-start(f32[13,1024,128]{2,1,0:T(8,128)S(1)} %get-tuple-element.17.b) | copy-start | bytes 20447236
  73.7 2.1 copy-start.5
  75.8 2.2 copy-start.6
  103.1 2.4 %copy-start.2 = (f32[11,1040,128]{2,1,0:T(8,128)}, f32[11,1040,128]{2,1,0:T(8,128)S(1)}, u32[]{:S(2)}) copy-start(f32[11,1040,128]{2,1,0:T(8,128)S(1)} %get-tuple-element.21.v1) | copy-start | bytes 17571844
  105.5 2.1 copy-start.3
  107.7 6.5 %collective-permute-start.11 = (f32[8,128]{1,0:T(8,128)S(1)}, f32[8,128]{1,0:T(8,128)S(1)}, u32[]{:S(2)}, u32[]{:S(2)}) collective-permute-start(f32[8,128]{1,0:T(8,128)S(1)} %get-tuple-element.18), channel_id=1, source_target_pairs={{0,6},{2,4},{4,2},{6,0},{8,14},{10,12},{12,10},{14,8},{16,22},{18,... | collective-permute-start | bytes 12296 | tf_op jit(solution)/shard_map/ppermute | solution.py:311
  112.6 4.0 %collective-permute-start.10 = (f32[8,128]{1,0:T(8,128)S(1)}, f32[8,128]{1,0:T(8,128)S(1)}, u32[]{:S(2)}, u32[]{:S(2)}) collective-permute-start(f32[8,128]{1,0:T(8,128)S(1)} %get-tuple-element.18), channel_id=1, source_target_pairs={{0,4},{2,6},{4,0},{6,2},{8,12},{10,14},{12,8},{14,10},{16,20},{18,... | collective-permute-start | bytes 12296 | tf_op jit(solution)/shard_map/ppermute | solution.py:311
  112.6 4.0 %collective-permute-start.9 = (f32[8,128]{1,0:T(8,128)S(1)}, f32[8,128]{1,0:T(8,128)S(1)}, u32[]{:S(2)}, u32[]{:S(2)}) collective-permute-start(f32[8,128]{1,0:T(8,128)S(1)} %get-tuple-element.18), channel_id=1, source_target_pairs={{0,2},{2,0},{4,6},{6,4},{8,10},{10,8},{12,14},{14,12},{16,18},{18,... | collective-permute-start | bytes 12296 | tf_op jit(solution)/shard_map/ppermute | solution.py:311
  116.6 5.4 %collective-permute-start.14 = (f32[8,128]{1,0:T(8,128)S(1)}, f32[8,128]{1,0:T(8,128)S(1)}, u32[]{:S(2)}, u32[]{:S(2)}) collective-permute-start(f32[8,128]{1,0:T(8,128)S(1)} %add_add_fusion.3), channel_id=1, source_target_pairs={{0,24},{2,26},{4,28},{6,30},{8,16},{10,18},{12,20},{14,22},{16,8},... | collective-permute-start | bytes 12296 | tf_op jit(solution)/shard_map/ppermute | solution.py:311
  121.0 4.0 %collective-permute-start.13 = (f32[8,128]{1,0:T(8,128)S(1)}, f32[8,128]{1,0:T(8,128)S(1)}, u32[]{:S(2)}, u32[]{:S(2)}) collective-permute-start(f32[8,128]{1,0:T(8,128)S(1)} %add_add_fusion.3), channel_id=1, source_target_pairs={{0,16},{2,18},{4,20},{6,22},{8,24},{10,26},{12,28},{14,30},{16,0},... | collective-permute-start | bytes 12296 | tf_op jit(solution)/shard_map/ppermute | solution.py:311
  121.0 4.0 %collective-permute-start.12 = (f32[8,128]{1,0:T(8,128)S(1)}, f32[8,128]{1,0:T(8,128)S(1)}, u32[]{:S(2)}, u32[]{:S(2)}) collective-permute-start(f32[8,128]{1,0:T(8,128)S(1)} %add_add_fusion.3), channel_id=1, source_target_pairs={{0,8},{2,10},{4,12},{6,14},{8,0},{10,2},{12,4},{14,6},{16,24},{18,... | collective-permute-start | bytes 12296 | tf_op jit(solution)/shard_map/ppermute | solution.py:311
  124.9 30.3 %copy-start.12 = (f32[1,128,128]{2,1,0:T(8,128)S(1)}, f32[1,128,128]{2,1,0:T(8,128)}, u32[]{:S(2)}) copy-start(f32[1,128,128]{2,1,0:T(8,128)} %pad_dynamic-slice_fusion.2) | copy-start | bytes 196612
  124.9 36.5 %copy-start.11 = (f32[3,2,128,128]{3,2,1,0:T(8,128)S(1)}, f32[3,2,128,128]{3,2,1,0:T(8,128)}, u32[]{:S(2)}) copy-start(f32[3,2,128,128]{3,2,1,0:T(8,128)} %param.13) | copy-start | bytes 1179652
  152.0 3.7 %collective-permute-start.17 = (f32[8,128]{1,0:T(8,128)S(1)}, f32[8,128]{1,0:T(8,128)S(1)}, u32[]{:S(2)}, u32[]{:S(2)}) collective-permute-start(f32[8,128]{1,0:T(8,128)S(1)} %get-tuple-element.25), channel_id=1, source_target_pairs={{0,6},{2,4},{4,2},{6,0},{8,14},{10,12},{12,10},{14,8},{16,22},{18,... | collective-permute-start | bytes 12296 | tf_op jit(solution)/shard_map/ppermute | solution.py:311
  154.1 4.0 %collective-permute-start.16 = (f32[8,128]{1,0:T(8,128)S(1)}, f32[8,128]{1,0:T(8,128)S(1)}, u32[]{:S(2)}, u32[]{:S(2)}) collective-permute-start(f32[8,128]{1,0:T(8,128)S(1)} %get-tuple-element.25), channel_id=1, source_target_pairs={{0,4},{2,6},{4,0},{6,2},{8,12},{10,14},{12,8},{14,10},{16,20},{18,... | collective-permute-start | bytes 12296 | tf_op jit(solution)/shard_map/ppermute | solution.py:311
  154.9 3.2 %collective-permute-start.15 = (f32[8,128]{1,0:T(8,128)S(1)}, f32[8,128]{1,0:T(8,128)S(1)}, u32[]{:S(2)}, u32[]{:S(2)}) collective-permute-start(f32[8,128]{1,0:T(8,128)S(1)} %get-tuple-element.25), channel_id=1, source_target_pairs={{0,2},{2,0},{4,6},{6,4},{8,10},{10,8},{12,14},{14,12},{16,18},{18,... | collective-permute-start | bytes 12296 | tf_op jit(solution)/shard_map/ppermute | solution.py:311
  158.1 4.0 %collective-permute-start.20 = (f32[8,128]{1,0:T(8,128)S(1)}, f32[8,128]{1,0:T(8,128)S(1)}, u32[]{:S(2)}, u32[]{:S(2)}) collective-permute-start(f32[8,128]{1,0:T(8,128)S(1)} %add_add_fusion.1), channel_id=1, source_target_pairs={{0,24},{2,26},{4,28},{6,30},{8,16},{10,18},{12,20},{14,22},{16,8},... | collective-permute-start | bytes 12296 | tf_op jit(solution)/shard_map/ppermute | solution.py:311
  158.5 4.0 %collective-permute-start.19 = (f32[8,128]{1,0:T(8,128)S(1)}, f32[8,128]{1,0:T(8,128)S(1)}, u32[]{:S(2)}, u32[]{:S(2)}) collective-permute-start(f32[8,128]{1,0:T(8,128)S(1)} %add_add_fusion.1), channel_id=1, source_target_pairs={{0,16},{2,18},{4,20},{6,22},{8,24},{10,26},{12,28},{14,30},{16,0},... | collective-permute-start | bytes 12296 | tf_op jit(solution)/shard_map/ppermute | solution.py:311
  159.7 2.7 %collective-permute-start.18 = (f32[8,128]{1,0:T(8,128)S(1)}, f32[8,128]{1,0:T(8,128)S(1)}, u32[]{:S(2)}, u32[]{:S(2)}) collective-permute-start(f32[8,128]{1,0:T(8,128)S(1)} %add_add_fusion.1), channel_id=1, source_target_pairs={{0,8},{2,10},{4,12},{6,14},{8,0},{10,2},{12,4},{14,6},{16,24},{18,... | collective-permute-start | bytes 12296 | tf_op jit(solution)/shard_map/ppermute | solution.py:311
  162.4 2.4 %copy-start.4 = (f32[9,1040,128]{2,1,0:T(8,128)S(1)}, f32[9,1040,128]{2,1,0:T(8,128)}, u32[]{:S(2)}) copy-start(f32[9,1040,128]{2,1,0:T(8,128)} %get-tuple-element.27.u0) | copy-start | bytes 14376964
  164.8 2.1 copy-start.7
  166.9 1.8 copy-start.8
  171.3 25.6 %all-to-all-start = ((f32[8,2,128,128]{3,2,1,0:T(8,128)}), f32[8,2,128,128]{3,2,1,0:T(8,128)S(1)}, u32[]{:S(2)}, u32[]{:S(2)}) async-start(f32[8,2,128,128]{3,2,1,0:T(8,128)} %gradient.1), calls=%async_computation | async-start | bytes 2097152 | tf_op jit(solution)/shard_map/all_to_all | solution.py:389
  181.8 35.1 %copy-start.15 = (pred[128]{0:T(512)(128)(4,1)S(1)}, pred[128]{0:T(512)(128)(4,1)}, u32[]{:S(2)}) copy-start(pred[128]{0:T(512)(128)(4,1)} %constant.64.clone.1) | copy-start | bytes 388
  181.9 36.7 %copy-start.10 = (f32[3,2,128,128]{3,2,1,0:T(8,128)}, f32[3,2,128,128]{3,2,1,0:T(8,128)S(1)}, u32[]{:S(2)}) copy-start(f32[3,2,128,128]{3,2,1,0:T(8,128)S(1)} %broadcast_divide_fusion) | copy-start | bytes 1179652
  182.0 34.8 %collective-permute-start.22 = (f32[2,1,128]{2,1,0:T(1,128)S(1)}, f32[2,1,128]{2,1,0:T(1,128)S(1)}, u32[]{:S(2)}, u32[]{:S(2)}) collective-permute-start(f32[2,1,128]{2,1,0:T(1,128)S(1)} %slice.95), channel_id=1, source_target_pairs={{0,32},{32,64},{64,96},{1,33},{33,65},{65,97},{2,34},{34,66},{66,9... | collective-permute-start | bytes 3080 | tf_op jit(solution)/shard_map/ppermute | solution.py:302
  196.9 1.0 copy-start.9
  199.9 15.5 %all-to-all-start.1 = ((f32[128,1,128]{2,1,0:T(1,128)}), f32[128,1,128]{2,1,0:T(1,128)S(1)}, u32[]{:S(2)}, u32[]{:S(2)}) async-start(f32[128,1,128]{2,1,0:T(1,128)} %bitcast.47), calls=%async_computation.1 | async-start | bytes 131072 | tf_op jit(solution)/shard_map/all_to_all | solution.py:397
  206.2 10.7 %collective-permute-start.21 = (f32[1,128,128]{2,1,0:T(8,128)S(1)}, f32[1,128,128]{2,1,0:T(8,128)S(1)}, u32[]{:S(2)}, u32[]{:S(2)}) collective-permute-start(f32[1,128,128]{2,1,0:T(8,128)S(1)} %get-tuple-element.38), channel_id=1, source_target_pairs={{0,1},{1,2},{2,3},{3,4},{4,5},{5,6},{6,7},{7,8},{8,9},{9,10},{10,1... | collective-permute-start | bytes 196616 | tf_op jit(solution)/shard_map/ppermute | solution.py:302

commit v2 on v1

v2 whole, which is shorter than its diff:
```python
import functools

import jax
import jax.numpy as jnp
from jax import lax
from jax.experimental import pallas as pl
from jax.experimental.pallas import tpu as pltpu
from jax.sharding import Mesh
from jax.sharding import PartitionSpec as P


HALF = 2
PLANES = 13
KEPT = 9
PAD = 8
ROWS = 1024

dual_step = 0.5
primal_step = 0.2
tv_weight = 0.5

VMEM = pl.BlockSpec(memory_space=pltpu.VMEM)
SMEM = pl.BlockSpec(memory_space=pltpu.SMEM)


def params(mib):
    return pltpu.CompilerParams(vmem_limit_bytes=mib * 2**20)


def spread_points(index, parts, right_planes, write):
    points = index.shape[1]
    column = (index >> 16) * 128 + (index & 127)
    row = ((index >> 7) & 511) - lax.broadcasted_iota(jnp.int32, (8, points), 0) // HALF
    lanes = lax.broadcasted_iota(jnp.int32, (right_planes * 128, points), 0)
    right = jnp.where(lanes == column, 1.0, 0.0).astype(jnp.bfloat16)
    tile = lax.broadcasted_iota(jnp.int32, (ROWS // 8, 8, points), 0)
    mask = row[None] == (8 // HALF) * tile
    for which, part in enumerate(parts):
        total = None
        for piece in part:
            left = jnp.where(mask, piece[None], 0.0).reshape(ROWS, points).astype(jnp.bfloat16)
            got = lax.dot_general(
                left, right, (((1,), (1,)), ((), ())), preferred_element_type=jnp.float32
            )
            total = got if total is None else total + got
        for p in range(right_planes):
            write(which, p, total[:, p * 128 : (p + 1) * 128])


def pieces_of(value, count):
    high = value.astype(jnp.bfloat16).astype(jnp.float32)
    return [high, value - high][:count]


def points_of(core, lists, first):
    points = lists.shape[1]
    parity = lax.broadcasted_iota(jnp.int32, (8, points), 0) % HALF
    even = jnp.where(core == 0, lists[first : first + 1], lists[first + 2 : first + 3])
    odd = jnp.where(core == 0, lists[first + 1 : first + 2], lists[first + 3 : first + 4])
    return jnp.where(parity == 0, even, odd)


def writer(stores):
    def write(which, p, value):
        ref, first = stores[which]
        ref[first + p] = value

    return write


def scatter_src(core, lists, count, store, first):
    amp = points_of(core, lists, 2)
    index = lists[0:1].astype(jnp.int32)
    spread_points(index, [pieces_of(amp, count)], 2, writer([(store, first)]))


def scatter_rec(core, lists, count, planes, ob, cn, first):
    obs = points_of(core, lists, 6)
    index = lists[1:2].astype(jnp.int32)
    parts = [pieces_of(obs, count), [jnp.ones_like(obs)]]
    spread_points(index, parts, planes, writer([(ob, first), (cn, first)]))


def scatter_own_kernel(core_ref, lists, b, ob, cn):
    core = core_ref[0]

    def body(h, _):
        scatter_src(core, lists[h], 2, b, 2 * h)
        scatter_rec(core, lists[h], 2, 2, ob, cn, 2 * h)
        return 0

    lax.fori_loop(0, 2, body, 0)


def scatter_src_kernel(core_ref, low, high, far, b, held):
    core = core_ref[0]
    for k, rows in enumerate((low[1], high[0], low[0], high[1], far[0])):
        held[k, 0:10] = rows

    def two(k, _):
        scatter_src(core, held[k, 0:10], 2, b, 2 + 2 * k)
        return 0

    def one(k, _):
        scatter_src(core, held[2 + k, 0:10], 1, b, jnp.where(k == 0, 0, 4 + 2 * k))
        return 0

    lax.fori_loop(0, 2, two, 0)
    lax.fori_loop(0, 3, one, 0)


def scatter_rec_kernel(core_ref, low, high, ob, cn, held):
    core = core_ref[0]
    for k, rows in enumerate((low[1], high[0])):
        held[k, 0:10] = rows

    def two(k, _):
        scatter_rec(core, held[k, 0:10], 2, 2, ob, cn, 2 * k)
        return 0

    lax.fori_loop(0, 2, two, 0)
    scatter_rec(core, high[1], 1, 1, ob, cn, 4)


def shift_matrix():
    i = lax.broadcasted_iota(jnp.int32, (128, 128), 0)
    j = lax.broadcasted_iota(jnp.int32, (128, 128), 1)
    return jnp.where(jnp.abs(i - j) == 1, 1.0, 0.0).astype(jnp.bfloat16)


def neighbours(ref, t):
    ext = ref[t]
    x = ext[PAD : PAD + ROWS]
    total = ROWS + 2 * PAD
    down = pltpu.roll(ext, HALF, 0)[PAD : PAD + ROWS]
    up = pltpu.roll(ext, total - HALF, 0)[PAD : PAD + ROWS]
    high = x.astype(jnp.bfloat16)
    low = (x - high.astype(jnp.float32)).astype(jnp.bfloat16)
    matrix = shift_matrix()
    along = jnp.dot(high, matrix, preferred_element_type=jnp.float32)
    along = along + jnp.dot(low, matrix, preferred_element_type=jnp.float32)
    return x, (down + up) + along


def fold(x):
    return jnp.sum(x.reshape(ROWS // 8, 8, 128), 0)


def walk(first, last, body, carry):
    return lax.fori_loop(first, last, body, carry)


INNER = pl.ds(PAD, 1024)


def advance(src, s_off, inv, i_off, dst, d_off, first, last, dots):
    def body(t, carry):
        x, q = neighbours(src, t - s_off)
        q = q + (src[t - s_off - 1, INNER, :] + src[t - s_off + 1, INNER, :])
        new = inv[t - i_off] * q
        dst[t - d_off, INNER, :] = new
        if not dots:
            return carry
        return carry[0] + fold(x * q), carry[1] + fold(new * q)

    zero = jnp.zeros((8, 128), jnp.float32)
    return walk(first, last, body, (zero, zero) if dots else 0)


def last_moment(src, off):
    def body(t, carry):
        x, q = neighbours(src, t - off)
        q = q + 2.0 * src[t - off + 1, INNER, :]
        return carry + fold(x * q)

    return walk(4, 8, body, jnp.zeros((8, 128), jnp.float32))


def clear_pads(*refs):
    for ref in refs:
        zero = jnp.zeros((8, 128), jnp.float32)
        for t in range(ref.shape[0]):
            ref[t, 0:PAD, :] = zero
            ref[t, ref.shape[1] - PAD :, :] = zero


def message(moments):
    sub = lax.broadcasted_iota(jnp.int32, (8, 128), 0)
    lane = lax.broadcasted_iota(jnp.int32, (8, 128), 1)
    out = jnp.zeros((8, 128), jnp.float32)
    for k, moment in enumerate(moments):
        for c in range(HALF):
            total = jnp.sum(jnp.where(sub % HALF == c, moment, 0.0))
            out = out + jnp.where((sub == k) & (lane == c), total, 0.0)
    return out


def coefficients(moments):
    m = [moments[k : k + 1, :] for k in range(6)]

    def product(p, shift):
        total = 0.0
        for i, a in enumerate(p):
            for j, b in enumerate(p):
                total = total + a * b * (m[i + j] - m[i + j + 1] if shift else m[i + j])
        return total

    one = jnp.ones_like(m[0])
    z, p, energy = [one], [one], m[0]
    x = [0.0 * one] * 3
    for it in range(3):
        stride = energy / product(p, True)
        x = [x[i] + (stride * p[i] if i < len(p) else 0.0) for i in range(3)]
        if it < 2:
            applied = [a - b for a, b in zip(p + [0.0 * one], [0.0 * one] + p)]
            z = [a - stride * b for a, b in zip(z + [0.0 * one], applied)]
            new = product(z, False)
            p = [a + new / energy * b for a, b in zip(z, p + [0.0 * one])]
            energy = new
    lane = lax.broadcasted_iota(jnp.int32, (1, 128), 1)
    sub = lax.broadcasted_iota(jnp.int32, (8, 128), 0)
    out = []
    for v in x:
        value = [jnp.sum(jnp.where(lane == c, v, 0.0)) for c in range(HALF)]
        out.append(jnp.where(sub % HALF == 0, value[0], value[1]))
    return out


def times(pattern, x):
    return (pattern[None] * x.reshape(ROWS // 8, 8, 128)).reshape(ROWS, 128)


def forward_kernel(par, own_m, own_t, near_m, near_t, b_own, b_near, inv, v0, v1, v2, msg):
    core = par[5]
    slabs = (
        (near_m, near_t, 0, 0, 2), (near_m, near_t, 0, 1, 2),
        (own_m, own_t, 0, 0, None), (own_m, own_t, 0, 1, None),
        (near_m, near_t, 2, 0, 3), (near_m, near_t, 2, 1, 3), (near_m, near_t, 4, 0, 4),
    )
    clear_pads(v0, v1, v2)
    for slab, (mine, theirs, base, h, flag) in enumerate(slabs):
        valid = 1.0 if flag is None else par[flag]
        planes = 1 if slab == 6 else 2

        def fill(p, _, mine=mine, theirs=theirs, base=base, h=h, valid=valid, slab=slab):
            sigma = jnp.where(core == float(h), mine[base + p], theirs[base + p])
            for c in range(HALF):
                inv[2 * slab + p, pl.ds(c, 512, stride=HALF), :] = valid / (6.0 + par[c] * sigma)
            return 0

        lax.fori_loop(0, planes, fill, 0)

    def start(b, off, dots):
        def body(t, carry):
            right = b[t - off]
            new = inv[t] * right
            v0[t, INNER, :] = new
            return carry + fold(new * right) if dots else carry

        return body

    zero = jnp.zeros((8, 128), jnp.float32)
    walk(0, 4, start(b_near, 0, False), 0)
    m0 = walk(4, 8, start(b_own, 4, True), zero)
    walk(8, 13, start(b_near, 4, False), 0)
    advance(v0, 0, inv, 0, v1, 1, 1, 4, False)
    m1, m2 = advance(v0, 0, inv, 0, v1, 1, 4, 8, True)
    advance(v0, 0, inv, 0, v1, 1, 8, 12, False)
    advance(v1, 1, inv, 0, v2, 2, 2, 4, False)
    m3, m4 = advance(v1, 1, inv, 0, v2, 2, 4, 8, True)
    advance(v1, 1, inv, 0, v2, 2, 8, 11, False)
    m5 = last_moment(v2, 2)
    msg[...] = message([m0, m1, m2, m3, m4, m5])


def adjoint_kernel(
    total, inv, v0, v1, v2, ob_own, cn_own, ob_near, cn_near, wave, u0, u1, u2, msg
):
    a = coefficients(total[...])

    def start(ob, cn, off, own):
        def body(t, carry):
            w = times(a[0], v0[t, INNER, :]) + times(a[1], v1[t - 1, INNER, :])
            w = w + times(a[2], v2[t - 2, INNER, :])
            right = cn[t - off] * w - ob[t - off]
            new = inv[t] * right
            u0[t, INNER, :] = new
            if not own:
                return carry
            wave[t - 4] = w
            return carry + fold(new * right)

        return body

    zero = jnp.zeros((8, 128), jnp.float32)
    walk(2, 4, start(ob_near, cn_near, 2, False), 0)
    m0 = walk(4, 8, start(ob_own, cn_own, 4, True), zero)
    walk(8, 11, start(ob_near, cn_near, 6, False), 0)
    advance(u0, 0, inv, 0, u1, 1, 3, 4, False)
    m1, m2 = advance(u0, 0, inv, 0, u1, 1, 4, 8, True)
    advance(u0, 0, inv, 0, u1, 1, 8, 10, False)
    m3, m4 = advance(u1, 1, inv, 0, u2, 2, 4, 8, True)
    advance(u1, 1, inv, 0, u2, 2, 8, 9, False)
    m5 = last_moment(u2, 2)
    msg[...] = message([m0, m1, m2, m3, m4, m5])


def gradient_kernel(other, spot, par, total, wave, u0, u1, u2, *rest):
    out, held = rest[-2:]
    a = coefficients(total[...])
    sub = lax.broadcasted_iota(jnp.int32, (8, 128), 0)
    square = jnp.where(sub % HALF == 0, par[0], par[1])
    a = [-square * v for v in a]
    core = 1 - spot[2] if other else spot[2]
    for p in range(2):
        t = 4 + 2 * core + p
        x = times(a[0], u0[t, INNER, :]) + times(a[1], u1[t - 1, INNER, :])
        x = x + times(a[2], u2[t - 2, INNER, :])
        held[...] = x * wave[t - 4]
        for band in range(4):
            at = band * 256
            both = held[pl.ds(at, 128, stride=HALF), :] + held[pl.ds(at + 1, 128, stride=HALF), :]
            out[band, p] = both if other else both + rest[0][band, p]


def power_kernel(parts, own, msg):
    g = (parts[0] + parts[1]) + (parts[2] + parts[3])
    own[...] = g
    msg[...] = jnp.full((128, 128), jnp.sum(g * g), jnp.float32)


def variation_kernel(spot, slow, own_t, near_t, dual, dual_next, base, send_x, send_y):
    lap, pair, core = spot[0], spot[1], spot[2]
    start = pl.multiple_of(lap * 128, 128)
    band = pl.ds(start, 128)
    after = pl.ds(pl.multiple_of(jnp.minimum(start + 128, 504), 8), 8)
    row = lax.broadcasted_iota(jnp.int32, (128, 128), 0)
    lane = lax.broadcasted_iota(jnp.int32, (128, 128), 1)
    last_y = (row == 127) & (lap == 3)
    last_z = lane == 127
    comps = []
    for p in range(2):
        here = slow[p, band, :]
        if p == 0:
            step_x = slow[1, band, :] - here
        else:
            step_x = jnp.where(core == 0, own_t[0, band, :], near_t[2, band, :]) - here
            step_x = jnp.where((core == 1) & (pair == 15), 0.0, step_x)
        rolled = pltpu.roll(here, 127, 0)
        step_y = jnp.where(row == 127, slow[p, after, :][0:1], rolled) - here
        step_y = jnp.where(last_y, 0.0, step_y)
        step_z = jnp.where(last_z, 0.0, pltpu.roll(here, 127, 1) - here)
        trial = [dual[k, p] + dual_step * step for k, step in enumerate((step_x, step_y, step_z))]
        magnitude = jnp.sqrt(trial[0] * trial[0] + trial[1] * trial[1] + trial[2] * trial[2])
        scale = jnp.maximum(1.0, magnitude / tv_weight)
        new = [x / scale for x in trial]
        for k in range(3):
            dual_next[k, p] = new[k]
        if p == 1:
            new[0] = jnp.where((core == 1) & (pair == 15), 0.0, new[0])
        new[1] = jnp.where(last_y, 0.0, new[1])
        new[2] = jnp.where(last_z, 0.0, new[2])
        comps.append(new)
    for p in range(2):
        x, y, z = comps[p]
        back = jnp.where(row == 0, 0.0, pltpu.roll(y, 1, 0)) - y
        back = back + (jnp.where(lane == 0, 0.0, pltpu.roll(z, 1, 1)) - z)
        back = back + (comps[0][0] - x if p == 1 else -x)
        base[p] = slow[p, band, :] - primal_step * back
        send_y[p] = y[120:128]
    send_x[0] = comps[1][0]


def model_kernel(cells, base, grad, power, prior_x, prior_y, model):
    total = power[0]
    for k in range(1, 16):
        total = total + power[k]
    total = jnp.sum(total, axis=0, keepdims=True)
    scale = 1.0 / jnp.sqrt(total / cells + 1e-06)
    row = lax.broadcasted_iota(jnp.int32, (128, 128), 0)
    for p in range(2):
        back = jnp.where(row == 0, prior_y[p][7:8], 0.0)
        if p == 0:
            back = back + prior_x[0]
        model[p] = base[p] - primal_step * (grad[p] * scale + back)


def cost(work):
    return pl.CostEstimate(flops=work * 10**9, bytes_accessed=10**6, transcendentals=0)


def struct(*shape):
    return jax.ShapeDtypeStruct(shape, jnp.float32)


def moved(x, axis, by):
    peers = lax.axis_size(axis)
    return lax.ppermute(x, axis, [(i, i + by) for i in range(peers) if 0 <= i + by < peers])


def swapped(x):
    return lax.ppermute(x, "core", [(0, 1), (1, 0)])


def pair_sum(x):
    for masks in ((1, 2, 3), (4, 8, 12)):
        x = x + sum(lax.ppermute(x, "pair", [(i, i ^ d) for i in range(16)]) for d in masks)
    return x


def on_device(slowness, damping, src_index, src_amp, rec_index, observed, dual):
    width_x, rows_y, depth_z = slowness.shape
    slab_cells = width_x * rows_y * depth_z
    lap, pair, core = (lax.axis_index(name) for name in ("lap", "pair", "core"))
    pairs = lax.axis_size("pair")
    offset = (pair * 2 + core) * slab_cells

    squared = damping * damping
    own_sq = lax.dynamic_slice_in_dim(squared, core * HALF, HALF)
    flags = jnp.stack([pair >= 1, pair + 1 < pairs, pair + 2 < pairs, core == 1])
    par = jnp.concatenate([own_sq, flags.astype(jnp.float32), jnp.zeros(2, jnp.float32)])
    core_in = core.astype(jnp.int32).reshape(1)

    index = jnp.stack([src_index - offset, rec_index - offset]).astype(jnp.float32)
    lists = jnp.concatenate([index, src_amp, observed])
    spot = jnp.stack([lap, pair, core, core]).astype(jnp.int32)
    lists, par, core_in, spot = lax.optimization_barrier((lists, par, core_in, spot))
    other = swapped(lists)
    both = jnp.where(core_in[0] == 0, jnp.stack([lists, other]), jnp.stack([other, lists]))
    low, high, far = (moved(both, "pair", by) for by in (1, -1, -2))
    first = slowness[:1]
    sigma, first, both = lax.optimization_barrier((slowness, first, both))
    around = [
        moved(sigma, "pair", 1),
        moved(sigma, "pair", -1),
        lax.ppermute(first, ("pair", "core"), [(2 * i, 2 * i - 4) for i in range(2, pairs)]),
    ]
    own_t = swapped(sigma)

    points = lists.shape[1]
    b_own, ob_own, cn_own = pl.pallas_call(
        scatter_own_kernel,
        out_shape=(struct(4, ROWS, 128),) * 3,
        in_specs=[SMEM, VMEM],
        out_specs=(VMEM,) * 3,
        compiler_params=params(24),
        cost_estimate=cost(10),
        name="scatter_own",
    )(core_in, both)
    low, high, far, b_own = lax.optimization_barrier((low, high, far, b_own))
    held = pltpu.VMEM((5, 16, points), jnp.float32)
    b_near = pl.pallas_call(
        scatter_src_kernel,
        out_shape=struct(10, ROWS, 128),
        in_specs=[SMEM] + [VMEM] * 3,
        out_specs=VMEM,
        scratch_shapes=[held],
        compiler_params=params(24),
        cost_estimate=cost(7),
        name="scatter_src",
    )(core_in, low, high, far)
    around, b_near = lax.optimization_barrier((around, b_near))
    near_m = jnp.concatenate(around)
    near_t = swapped(near_m)
    near_m, low = lax.optimization_barrier((near_m, low))
    ob_near, cn_near = pl.pallas_call(
        scatter_rec_kernel,
        out_shape=(struct(5, ROWS, 128),) * 2,
        in_specs=[SMEM] + [VMEM] * 2,
        out_specs=(VMEM,) * 2,
        scratch_shapes=[held],
        compiler_params=params(24),
        cost_estimate=cost(8),
        name="scatter_rec",
    )(core_in, low, high)
    near_t, ob_near = lax.optimization_barrier((near_t, ob_near))

    padded = ROWS + 2 * PAD
    inv, v0, v1, v2, msg = pl.pallas_call(
        forward_kernel,
        out_shape=(
            struct(PLANES, ROWS, 128), struct(13, padded, 128), struct(11, padded, 128),
            struct(9, padded, 128), struct(8, 128),
        ),
        in_specs=[SMEM] + [VMEM] * 6,
        out_specs=(VMEM,) * 5,
        compiler_params=params(8),
        cost_estimate=cost(20),
        name="forward",
    )(par, slowness, own_t, near_m, near_t, b_own, b_near)

    wave, u0, u1, u2, msg = pl.pallas_call(
        adjoint_kernel,
        out_shape=(
            struct(4, ROWS, 128), struct(13, padded, 128), struct(11, padded, 128),
            struct(9, padded, 128), struct(8, 128),
        ),
        in_specs=[VMEM] * 9,
        out_specs=(VMEM,) * 5,
        input_output_aliases={2: 1, 3: 2, 4: 3},
        compiler_params=params(8),
        cost_estimate=cost(14),
        name="adjoint",
    )(pair_sum(msg), inv, v0, v1, v2, ob_own, cn_own, ob_near, cn_near)

    total = pair_sum(msg)

    def gradient(other, *more):
        return pl.pallas_call(
            functools.partial(gradient_kernel, other),
            out_shape=struct(4, 2, 128, 128),
            in_specs=[SMEM, SMEM] + [VMEM] * (5 + len(more)),
            out_specs=VMEM,
            scratch_shapes=[pltpu.VMEM((ROWS, 128), jnp.float32)],
            compiler_params=params(8),
            name="gradient",
        )(spot, par, total, wave, u0, u1, u2, *more)

    parts = gradient(False, swapped(gradient(True)))
    slowness, dual, own_t, near_t, parts = lax.optimization_barrier(
        (slowness, dual, own_t, near_t, parts)
    )
    arrived = lax.all_to_all(parts, "lap", 0, 0, tiled=True)
    dual_next, base, send_x, send_y = pl.pallas_call(
        variation_kernel,
        out_shape=(
            struct(3, 2, 128, 128), struct(2, 128, 128), struct(1, 128, 128), struct(2, 8, 128),
        ),
        in_specs=[SMEM] + [VMEM] * 4,
        out_specs=(VMEM,) * 4,
        compiler_params=params(8),
        cost_estimate=cost(1),
        name="variation",
    )(spot, slowness, own_t, near_t, dual)
    own_grad, power = pl.pallas_call(
        power_kernel,
        out_shape=(struct(2, 128, 128), struct(128, 128)),
        in_specs=[VMEM],
        out_specs=(VMEM, VMEM),
        compiler_params=params(8),
        name="power",
    )(arrived)
    power = lax.all_to_all(power, ("lap", "pair", "core"), 0, 0, tiled=True)
    prior_x = moved(send_x, ("pair", "core"), 1)
    prior_y = moved(send_y, "lap", 1)
    model = pl.pallas_call(
        functools.partial(model_kernel, float(slab_cells * 2 * pairs)),
        out_shape=struct(2, 128, 128),
        in_specs=[VMEM] * 5,
        out_specs=VMEM,
        compiler_params=params(8),
        name="model",
    )(base, own_grad, power.reshape(16, 8, 128), prior_x, prior_y)
    return (model, dual_next)


def solution(mesh):
    space = mesh.devices.shape[1]
    mesh = Mesh(mesh.devices.reshape(-1, space // 2, 2), ("lap", "pair", "core"))
    both = ("pair", "core")
    in_specs = (
        P(both, None, None),
        P("lap"),
        P(both),
        P("lap", both),
        P(both),
        P("lap", both),
        P(None, both, "lap", None),
    )
    out_specs = (P(both, "lap", None), P(None, both, "lap", None))
    return jax.shard_map(
        on_device, mesh=mesh, in_specs=in_specs, out_specs=out_specs, check_vma=False
    )
```

time: 219 us -> 135 us (0.62)
  Pallas kernels: 81.7 us -> 42.6 us
  waiting for transfers between devices: 48.5 us -> 20.3 us
  local copies, waits for them, and re-layouts: 23.1 us -> 2.64 us
  starting transfers between devices: 58.4 us -> 65.4 us
  other arithmetic: 5.23 us -> 2.48 us
    pallas_call x4 -> x9, Pallas kernels: 79.6 us -> 41.8 us  [the longest x1 12 us: on_device(): pl.pallas_call(forward_kernel, out_shape=(struct(PLANES, ROWS, 128), stru...]
    ppermute x8 -> x7, waiting for transfers between devices: 21.6 us -> 0.79 us  [moved(): lax.ppermute(x, axis, [(i, i + by) for i in range(peers) if 0 <= i + by <...]
    unnamed x34 -> x18, local copies, waits for them, and re-layouts: 18.8 us -> 1.58 us
    ppermute x3 -> x4, starting transfers between devices: 2.86 us -> 17.7 us  [swapped(): return lax.ppermute(x, 'core', [(0, 1), (1, 0)])]
    all_to_all x1, waiting for transfers between devices: 11.5 us -> 3.28 us  [on_device(): arrived = lax.all_to_all(parts, 'lap', 0, 0, tiled=True)]
    all_to_all x1, starting transfers between devices: 10.5 us -> 4.02 us  [on_device(): arrived = lax.all_to_all(parts, 'lap', 0, 0, tiled=True)]
    sub x2 -> x0, other arithmetic: 2.45 us -> none  [the longest x1 1.69 us: on_device(): model = own_model - primal_step * (scaled + back_x + back_y + back_z)]
    ppermute x8 -> x7, starting transfers between devices: 21.6 us -> 20.4 us  [moved(): lax.ppermute(x, axis, [(i, i + by) for i in range(peers) if 0 <= i + by <...]
  transfers between devices with their start and end apart: 25 -> 26, of which waited for: 13 -> 13; matrix products, arithmetic and copies ran while one was open for 4% -> 1% of each run, Pallas kernels for 12% -> 13%
where the time goes in v2:
time: 135 us; the launch traced here: 134 us
  starting transfers between devices  65.4 us (48%)
  Pallas kernels  42.6 us (32%)
  waiting for transfers between devices  20.3 us (15%)
  local copies, waits for them, and re-layouts  2.64 us (2%)
  other arithmetic  2.48 us (2%)
    ppermute x7, starting transfers between devices, moved(): lax.ppermute(x, axis, [(i, i + by) for i in range(peers) if 0 <= i + by <...  20.4 us
    ppermute x4, starting transfers between devices, swapped(): return lax.ppermute(x, 'core', [(0, 1), (1, 0)])  17.7 us
    ppermute x12, starting transfers between devices, pair_sum(): lax.ppermute(x, 'pair', [(i, i ^ d) for i in range(16)])  15.5 us
    pallas_call x1, Pallas kernels, on_device(): pl.pallas_call(forward_kernel, out_shape=(struct(PLANES, ROWS, 128), stru...  12 us
    ppermute x12, waiting for transfers between devices, pair_sum(): lax.ppermute(x, 'pair', [(i, i ^ d) for i in range(16)])  9.44 us
    pallas_call x1, Pallas kernels, on_device(): pl.pallas_call(adjoint_kernel, out_shape=(struct(4, ROWS, 128), struct(13...  8.68 us
    all_to_all x1, starting transfers between devices, on_device(): power = lax.all_to_all(power, ('lap', 'pair', 'core'), 0, 0, tiled=True)  7.16 us
    pallas_call x1, Pallas kernels, on_device(): pl.pallas_call(scatter_own_kernel, out_shape=(struct(4, ROWS, 128),) * 3,...  5.85 us
  transfers between devices with their start and end apart: 26, of which 13 were waited for; matrix products, arithmetic and copies ran while one was open for 1% of the time, Pallas kernels for 13%

profile of v2, /device:TPU:1, one launch (start us, length us, event | category | flops | bytes accessed | tf_op | source)
XLA Modules:
  0.0 134.4 jit_solution(17826833475815637338)
XLA Ops:
  0.6 0.7 mul.14
  1.5 0.7 broadcast_subtract_fusion
  2.4 0.8 pad_maximum_fusion
  3.2 1.5 %collective-permute-start = (f32[10,1024]{1,0:T(8,128)S(1)}, f32[10,1024]{1,0:T(8,128)S(1)}, u32[]{:S(2)}, u32[]{:S(2)}) collective-permute-start(f32[10,1024]{1,0:T(8,128)S(1)} %pad_maximum_fusion), channel_id=1, source_target_pairs={{0,1},{1,0},{2,3},{3,2},{4,5},{5,4},{6,7},{7,6},{8,9},{9,8},{10,11... | collective-permute-start | bytes 122888 | tf_op jit(solution)/shard_map/ppermute | solution.py:402
  4.7 1.0 slice.3
  5.7 1.3 collective-permute-start.7
  7.0 1.3 collective-permute-start.6
  8.3 4.3 %collective-permute-start.5 = (f32[2,10,1024]{2,1,0:T(8,128)S(1)}, f32[2,10,1024]{2,1,0:T(8,128)S(1)}, u32[]{:S(2)}, u32[]{:S(2)}) collective-permute-start(f32[2,10,1024]{2,1,0:T(8,128)S(1)} %maximum_select_fusion.lists), channel_id=1, source_target_pairs={{0,2},{2,4},{4,6},{6,8},{8,10},{10,12},{12,14},{14,16},{16,18},{18... | collective-permute-start | bytes 245768 | tf_op jit(solution)/shard_map/ppermute | solution.py:398
  12.6 1.3 collective-permute-start.3
  13.9 4.8 %collective-permute-start.2 = (f32[2,512,128]{2,1,0:T(8,128)}, f32[2,512,128]{2,1,0:T(8,128)S(1)}, u32[]{:S(2)}, u32[]{:S(2)}) collective-permute-start(f32[2,512,128]{2,1,0:T(8,128)} %slow), channel_id=1, source_target_pairs={{0,2},{2,4},{4,6},{6,8},{8,10},{10,12},{12,14},{14,16},{16,18},{18... | collective-permute-start | bytes 1572872 | tf_op jit(solution)/shard_map/ppermute | solution.py:398
  18.7 5.8 %scatter_own.1 = (f32[4,1024,128]{2,1,0:T(8,128)S(1)}, f32[4,1024,128]{2,1,0:T(8,128)S(1)}, f32[4,1024,128]{2,1,0:T(8,128)S(1)}) custom-call(s32[1]{0:T(128)} %bitcast.6.core_ref, f32[2,10,1024]{2,1,0:T(8,128)S(1)} %maximum_select_fusion.lists), custom_call_target="tpu_custom_call" | custom-call | flops 10000000000 | bytes 1000000 | tf_op jit(solution)/shard_map/scatter_own/pallas_call | solution.py:441
  24.6 0.7 collective-permute-start.4
  25.3 4.9 %scatter_src.1.b_near = f32[10,1024,128]{2,1,0:T(8,128)S(1)} custom-call(s32[1]{0:T(128)} %bitcast.6.core_ref, f32[2,10,1024]{2,1,0:T(8,128)S(1)} %collective-permute-done.5.low, f32[2,10,1024]{2,1,0:T(8,128)S(1)} %collective-permute-done.6.high, f32[2,10,1024]{2,1,0:T(8,128)S(1)} %collective-permute-done.7.far), custom_call_target="tpu_custom_call" | custom-call | flops 7000000000 | bytes 1000000 | tf_op jit(solution)/shard_map/scatter_src/pallas_call | solution.py:452
  30.3 9.9 %collective-permute-start.8 = (f32[5,512,128]{2,1,0:T(8,128)S(1)}, f32[5,512,128]{2,1,0:T(8,128)S(1)}, u32[]{:S(2)}, u32[]{:S(2)}) collective-permute-start(f32[5,512,128]{2,1,0:T(8,128)S(1)} %constant_dynamic-update-slice_fusion.near_m), channel_id=1, source_target_pairs={{0,1},{1,0},{2,3},{3,2},{4,5},{5,4},{6,7},{7,6},{8,9},{9,8},{10,11... | collective-permute-start | bytes 3932168 | tf_op jit(solution)/shard_map/ppermute | solution.py:402
  40.3 4.9 %scatter_rec.1 = (f32[5,1024,128]{2,1,0:T(8,128)S(1)}, f32[5,1024,128]{2,1,0:T(8,128)S(1)}) custom-call(s32[1]{0:T(128)} %bitcast.6.core_ref, f32[2,10,1024]{2,1,0:T(8,128)S(1)} %collective-permute-done.5.low, f32[2,10,1024]{2,1,0:T(8,128)S(1)} %collective-permute-done.6.high), custom_call_target="tpu_custom_call" | custom-call | flops 8000000000 | bytes 1000000 | tf_op jit(solution)/shard_map/scatter_rec/pallas_call | solution.py:466
  45.3 1.5 %copy-done.2 = f32[5,1024,128]{2,1,0:T(8,128)} copy-done((f32[5,1024,128]{2,1,0:T(8,128)}, f32[5,1024,128]{2,1,0:T(8,128)S(1)}, u32[]{:S(2)}) %copy-start.2) | copy-done | bytes 2621464
  46.8 12.0 %forward.1 = (f32[13,1024,128]{2,1,0:T(8,128)S(1)}, f32[13,1040,128]{2,1,0:T(8,128)S(1)}, f32[11,1040,128]{2,1,0:T(8,128)S(1)}, f32[9,1040,128]{2,1,0:T(8,128)S(1)}, f32[8,128]{1,0:T(8,128)S(1)}) custom-call(f32[8]{0:T(128)S(1)} %pad_maximum_fusion.1.par, f32[2,512,128]{2,1,0:T(8,128)S(1)} %copy-done, f32[2,512,128]{2,1,0:T(8,128)S(1)} %collective-permute-done.1.own_t, ...), custom_call_target="tpu_custom_call" | custom-call | flops 20000000000 | bytes 1000000 | tf_op jit(solution)/shard_map/forward/pallas_call | solution.py:479
  58.8 4.8 %collective-permute-start.11 = (f32[8,128]{1,0:T(8,128)S(1)}, f32[8,128]{1,0:T(8,128)S(1)}, u32[]{:S(2)}, u32[]{:S(2)}) collective-permute-start(f32[8,128]{1,0:T(8,128)S(1)} %get-tuple-element.67), channel_id=1, source_target_pairs={{0,6},{2,4},{4,2},{6,0},{8,14},{10,12},{12,10},{14,8},{16,22},{18,... | collective-permute-start | bytes 12296 | tf_op jit(solution)/shard_map/ppermute | solution.py:407
  63.6 0.7 collective-permute-start.9
  64.6 3.0 %collective-permute-done.10 = f32[8,128]{1,0:T(8,128)S(1)} collective-permute-done((f32[8,128]{1,0:T(8,128)S(1)}, f32[8,128]{1,0:T(8,128)S(1)}, u32[]{:S(2)}, u32[]{:S(2)}) %collective-permute-start.10) | collective-permute-done | bytes 4128 | tf_op jit(solution)/shard_map/ppermute | solution.py:407
  67.5 1.2 collective-permute-start.14
  68.8 1.9 %collective-permute-start.13 = (f32[8,128]{1,0:T(8,128)S(1)}, f32[8,128]{1,0:T(8,128)S(1)}, u32[]{:S(2)}, u32[]{:S(2)}) collective-permute-start(f32[8,128]{1,0:T(8,128)S(1)} %add_add_fusion.3), channel_id=1, source_target_pairs={{0,16},{2,18},{4,20},{6,22},{8,24},{10,26},{12,28},{14,30},{16,0},... | collective-permute-start | bytes 12296 | tf_op jit(solution)/shard_map/ppermute | solution.py:407
  71.3 1.5 %collective-permute-done.13 = f32[8,128]{1,0:T(8,128)S(1)} collective-permute-done((f32[8,128]{1,0:T(8,128)S(1)}, f32[8,128]{1,0:T(8,128)S(1)}, u32[]{:S(2)}, u32[]{:S(2)}) %collective-permute-start.13) | collective-permute-done | bytes 4128 | tf_op jit(solution)/shard_map/ppermute | solution.py:407
  72.7 0.7 collective-permute-done.12
  73.5 8.7 %adjoint.1 = (f32[4,1024,128]{2,1,0:T(8,128)S(1)}, f32[13,1040,128]{2,1,0:T(8,128)S(1)}, f32[11,1040,128]{2,1,0:T(8,128)S(1)}, f32[9,1040,128]{2,1,0:T(8,128)S(1)}, f32[8,128]{1,0:T(8,128)S(1)}) custom-call(f32[8,128]{1,0:T(8,128)S(1)} %add_add_fusion.2.total, ...), custom_call_target="tpu_custom_call", output_to_operand_aliasing={{1}: (2, {}), {2}: (3, {}), {3}: (4, {})} | custom-call | flops 14000000000 | bytes 1000000 | tf_op jit(solution)/shard_map/adjoint/pallas_call | solution.py:492
  82.2 1.4 %collective-permute-start.17 = (f32[8,128]{1,0:T(8,128)S(1)}, f32[8,128]{1,0:T(8,128)S(1)}, u32[]{:S(2)}, u32[]{:S(2)}) collective-permute-start(f32[8,128]{1,0:T(8,128)S(1)} %get-tuple-element.76), channel_id=1, source_target_pairs={{0,6},{2,4},{4,2},{6,0},{8,14},{10,12},{12,10},{14,8},{16,22},{18,... | collective-permute-start | bytes 12296 | tf_op jit(solution)/shard_map/ppermute | solution.py:407
  83.6 0.8 collective-permute-start.16
  84.4 1.1 collective-permute-start.15
  85.9 1.7 %collective-permute-done.16 = f32[8,128]{1,0:T(8,128)S(1)} collective-permute-done((f32[8,128]{1,0:T(8,128)S(1)}, f32[8,128]{1,0:T(8,128)S(1)}, u32[]{:S(2)}, u32[]{:S(2)}) %collective-permute-start.16) | collective-permute-done | bytes 4128 | tf_op jit(solution)/shard_map/ppermute | solution.py:407
  87.6 0.9 collective-permute-start.20
  88.4 0.9 collective-permute-start.19
  89.3 1.6 %collective-permute-start.18 = (f32[8,128]{1,0:T(8,128)S(1)}, f32[8,128]{1,0:T(8,128)S(1)}, u32[]{:S(2)}, u32[]{:S(2)}) collective-permute-start(f32[8,128]{1,0:T(8,128)S(1)} %add_add_fusion.1), channel_id=1, source_target_pairs={{0,8},{2,10},{4,12},{6,14},{8,0},{10,2},{12,4},{14,6},{16,24},{18,... | collective-permute-start | bytes 12296 | tf_op jit(solution)/shard_map/ppermute | solution.py:407
  90.9 0.7 collective-permute-done.20
  91.6 0.8 collective-permute-done.19
  92.4 1.3 gradient.2
  93.7 6.2 %collective-permute-start.21 = (f32[4,2,128,128]{3,2,1,0:T(8,128)S(1)}, f32[4,2,128,128]{3,2,1,0:T(8,128)S(1)}, u32[]{:S(2)}, u32[]{:S(2)}) collective-permute-start(f32[4,2,128,128]{3,2,1,0:T(8,128)S(1)} %gradient.2), channel_id=1, source_target_pairs={{0,1},{1,0},{2,3},{3,2},{4,5},{5,4},{6,7},{7,6},{8,9},{9,8},{10,11... | collective-permute-start | bytes 1572872 | tf_op jit(solution)/shard_map/ppermute | solution.py:402
  99.9 1.5 %collective-permute-done.21.rest_0_ = f32[4,2,128,128]{3,2,1,0:T(8,128)S(1)} collective-permute-done((f32[4,2,128,128]{3,2,1,0:T(8,128)S(1)}, f32[4,2,128,128]{3,2,1,0:T(8,128)S(1)}, u32[]{:S(2)}, u32[]{:S(2)}) %collective-permute-start.21) | collective-permute-done | bytes 524320 | tf_op jit(solution)/shard_map/ppermute | solution.py:402
  101.4 2.1 %gradient.3 = f32[4,2,128,128]{3,2,1,0:T(8,128)} custom-call(s32[4]{0:T(128)S(1)} %pad_add_fusion.spot, f32[8]{0:T(128)S(1)} %pad_maximum_fusion.1.par, f32[8,128]{1,0:T(8,128)S(1)} %add_add_fusion.total, f32[4,1024,128]{2,1,0:T(8,128)S(1)} %get-tuple-element.77.wave, f32[13,1040,128]{2,1,0:T(8,128)S(1)} %get-tuple-element.78.u0, ...), custom_call_target="tpu_custom_call" | custom-call | tf_op jit(solution)/shard_map/gradient/pallas_call | solution.py:509
  103.5 4.0 %all-to-all-start = ((f32[4,2,128,128]{3,2,1,0:T(8,128)}), f32[4,2,128,128]{3,2,1,0:T(8,128)S(1)}, u32[]{:S(2)}, u32[]{:S(2)}) async-start(f32[4,2,128,128]{3,2,1,0:T(8,128)} %gradient.3), calls=%async_computation | async-start | bytes 1048576 | tf_op jit(solution)/shard_map/all_to_all | solution.py:523
  107.5 1.5 %variation.1 = (f32[3,2,128,128]{3,2,1,0:T(8,128)}, f32[2,128,128]{2,1,0:T(8,128)S(1)}, f32[1,128,128]{2,1,0:T(8,128)S(1)}, f32[2,8,128]{2,1,0:T(8,128)S(1)}) custom-call(s32[4]{0:T(128)S(1)} %pad_add_fusion.spot, f32[2,512,128]{2,1,0:T(8,128)S(1)} %copy-done, f32[2,512,128]{2,1,0:T(8,128)S(1)} %collective-permute-done.1.own_t, ...), custom_call_target="tpu_custom_call" | custom-call | flops 1000000000 | bytes 1000000 | tf_op jit(solution)/shard_map/variation/pallas_call | solution.py:524
  109.0 4.1 %collective-permute-start.22 = (f32[1,128,128]{2,1,0:T(8,128)S(1)}, f32[1,128,128]{2,1,0:T(8,128)S(1)}, u32[]{:S(2)}, u32[]{:S(2)}) collective-permute-start(f32[1,128,128]{2,1,0:T(8,128)S(1)} %get-tuple-element.89), channel_id=1, source_target_pairs={{0,1},{1,2},{2,3},{3,4},{4,5},{5,6},{6,7},{7,8},{8,9},{9,10},{10,1... | collective-permute-start | bytes 196616 | tf_op jit(solution)/shard_map/ppermute | solution.py:398
  113.1 3.3 %all-to-all-done.parts = f32[4,2,128,128]{3,2,1,0:T(8,128)S(1)} async-done(((f32[4,2,128,128]{3,2,1,0:T(8,128)}), f32[4,2,128,128]{3,2,1,0:T(8,128)S(1)}, u32[]{:S(2)}, u32[]{:S(2)}) %all-to-all-start) | async-done | bytes 524320 | tf_op jit(solution)/shard_map/all_to_all | solution.py:523
  116.4 0.8 power.1
  117.2 7.2 %all-to-all-start.1 = ((f32[128,1,128]{2,1,0:T(1,128)}), f32[128,1,128]{2,1,0:T(1,128)S(1)}, u32[]{:S(2)}, u32[]{:S(2)}) async-start(f32[128,1,128]{2,1,0:T(1,128)} %bitcast.13), calls=%async_computation.1 | async-start | bytes 131072 | tf_op jit(solution)/shard_map/all_to_all | solution.py:543
  124.4 3.3 %collective-permute-start.23 = (f32[2,8,128]{2,1,0:T(8,128)S(1)}, f32[2,8,128]{2,1,0:T(8,128)S(1)}, u32[]{:S(2)}, u32[]{:S(2)}) collective-permute-start(f32[2,8,128]{2,1,0:T(8,128)S(1)} %get-tuple-element.90), channel_id=1, source_target_pairs={{0,32},{32,64},{64,96},{1,33},{33,65},{65,97},{2,34},{34,66},{66,9... | collective-permute-start | bytes 24584 | tf_op jit(solution)/shard_map/ppermute | solution.py:398
  127.7 0.8 collective-permute-done.23.prior_y
  128.4 5.2 %all-to-all-done.1 = f32[128,1,128]{2,1,0:T(1,128)S(1)} async-done(((f32[128,1,128]{2,1,0:T(1,128)}), f32[128,1,128]{2,1,0:T(1,128)S(1)}, u32[]{:S(2)}, u32[]{:S(2)}) %all-to-all-start.1) | async-done | bytes 65568 | tf_op jit(solution)/shard_map/all_to_all | solution.py:543
  133.7 0.7 model.1
  (48 shorter events, 1.9 us)
Async XLA Ops:
  3.2 2.5 %collective-permute-start = (f32[10,1024]{1,0:T(8,128)S(1)}, f32[10,1024]{1,0:T(8,128)S(1)}, u32[]{:S(2)}, u32[]{:S(2)}) collective-permute-start(f32[10,1024]{1,0:T(8,128)S(1)} %pad_maximum_fusion), channel_id=1, source_target_pairs={{0,1},{1,0},{2,3},{3,2},{4,5},{5,4},{6,7},{7,6},{8,9},{9,8},{10,11... | collective-permute-start | bytes 122888 | tf_op jit(solution)/shard_map/ppermute | solution.py:402
  5.7 18.9 %collective-permute-start.7 = (f32[2,10,1024]{2,1,0:T(8,128)S(1)}, f32[2,10,1024]{2,1,0:T(8,128)S(1)}, u32[]{:S(2)}, u32[]{:S(2)}) collective-permute-start(f32[2,10,1024]{2,1,0:T(8,128)S(1)} %maximum_select_fusion.lists), channel_id=1, source_target_pairs={{4,0},{6,2},{8,4},{10,6},{12,8},{14,10},{16,12},{18,14},{20,16},{2... | collective-permute-start | bytes 245768 | tf_op jit(solution)/shard_map/ppermute | solution.py:398
  7.0 18.3 %collective-permute-start.6 = (f32[2,10,1024]{2,1,0:T(8,128)S(1)}, f32[2,10,1024]{2,1,0:T(8,128)S(1)}, u32[]{:S(2)}, u32[]{:S(2)}) collective-permute-start(f32[2,10,1024]{2,1,0:T(8,128)S(1)} %maximum_select_fusion.lists), channel_id=1, source_target_pairs={{2,0},{4,2},{6,4},{8,6},{10,8},{12,10},{14,12},{16,14},{18,16},{20... | collective-permute-start | bytes 245768 | tf_op jit(solution)/shard_map/ppermute | solution.py:398
  8.3 17.0 %collective-permute-start.5 = (f32[2,10,1024]{2,1,0:T(8,128)S(1)}, f32[2,10,1024]{2,1,0:T(8,128)S(1)}, u32[]{:S(2)}, u32[]{:S(2)}) collective-permute-start(f32[2,10,1024]{2,1,0:T(8,128)S(1)} %maximum_select_fusion.lists), channel_id=1, source_target_pairs={{0,2},{2,4},{4,6},{6,8},{8,10},{10,12},{12,14},{14,16},{16,18},{18... | collective-permute-start | bytes 245768 | tf_op jit(solution)/shard_map/ppermute | solution.py:398
  12.6 17.6 %collective-permute-start.3 = (f32[2,512,128]{2,1,0:T(8,128)}, f32[2,512,128]{2,1,0:T(8,128)S(1)}, u32[]{:S(2)}, u32[]{:S(2)}) collective-permute-start(f32[2,512,128]{2,1,0:T(8,128)} %slow), channel_id=1, source_target_pairs={{2,0},{4,2},{6,4},{8,6},{10,8},{12,10},{14,12},{16,14},{18,16},{20... | collective-permute-start | bytes 1572872 | tf_op jit(solution)/shard_map/ppermute | solution.py:398
  13.9 16.4 %collective-permute-start.2 = (f32[2,512,128]{2,1,0:T(8,128)}, f32[2,512,128]{2,1,0:T(8,128)S(1)}, u32[]{:S(2)}, u32[]{:S(2)}) collective-permute-start(f32[2,512,128]{2,1,0:T(8,128)} %slow), channel_id=1, source_target_pairs={{0,2},{2,4},{4,6},{6,8},{8,10},{10,12},{12,14},{14,16},{16,18},{18... | collective-permute-start | bytes 1572872 | tf_op jit(solution)/shard_map/ppermute | solution.py:398
  24.6 5.6 %copy-start.4 = (f32[4,1024,128]{2,1,0:T(8,128)}, f32[4,1024,128]{2,1,0:T(8,128)S(1)}, u32[]{:S(2)}) copy-start(f32[4,1024,128]{2,1,0:T(8,128)S(1)} %get-tuple-element.72.ob_own) | copy-start | bytes 6291460
  24.6 5.6 %copy-start.6 = (f32[4,1024,128]{2,1,0:T(8,128)}, f32[4,1024,128]{2,1,0:T(8,128)S(1)}, u32[]{:S(2)}) copy-start(f32[4,1024,128]{2,1,0:T(8,128)S(1)} %get-tuple-element.73.cn_own) | copy-start | bytes 6291460
  24.6 5.6 %collective-permute-start.4 = (f32[1,512,128]{2,1,0:T(8,128)S(1)}, f32[1,512,128]{2,1,0:T(8,128)S(1)}, u32[]{:S(2)}, u32[]{:S(2)}) collective-permute-start(f32[1,512,128]{2,1,0:T(8,128)S(1)} %slice.3), channel_id=1, source_target_pairs={{4,0},{6,2},{8,4},{10,6},{12,8},{14,10},{16,12},{18,14},{20,16},{2... | collective-permute-start | bytes 786440 | tf_op jit(solution)/shard_map/ppermute | solution.py:436
  30.2 10.1 %copy-start = (f32[2,512,128]{2,1,0:T(8,128)S(1)}, f32[2,512,128]{2,1,0:T(8,128)}, u32[]{:S(2)}) copy-start(f32[2,512,128]{2,1,0:T(8,128)} %slow) | copy-start | bytes 1572868
  30.3 16.4 %collective-permute-start.8 = (f32[5,512,128]{2,1,0:T(8,128)S(1)}, f32[5,512,128]{2,1,0:T(8,128)S(1)}, u32[]{:S(2)}, u32[]{:S(2)}) collective-permute-start(f32[5,512,128]{2,1,0:T(8,128)S(1)} %constant_dynamic-update-slice_fusion.near_m), channel_id=1, source_target_pairs={{0,1},{1,0},{2,3},{3,2},{4,5},{5,4},{6,7},{7,6},{8,9},{9,8},{10,11... | collective-permute-start | bytes 3932168 | tf_op jit(solution)/shard_map/ppermute | solution.py:402
  40.2 6.5 %collective-permute-start.1 = (f32[2,512,128]{2,1,0:T(8,128)S(1)}, f32[2,512,128]{2,1,0:T(8,128)S(1)}, u32[]{:S(2)}, u32[]{:S(2)}) collective-permute-start(f32[2,512,128]{2,1,0:T(8,128)S(1)} %copy-done), channel_id=1, source_target_pairs={{0,1},{1,0},{2,3},{3,2},{4,5},{5,4},{6,7},{7,6},{8,9},{9,8},{10,11... | collective-permute-start | bytes 1572872 | tf_op jit(solution)/shard_map/ppermute | solution.py:402
  45.3 1.5 %copy-start.2 = (f32[5,1024,128]{2,1,0:T(8,128)}, f32[5,1024,128]{2,1,0:T(8,128)S(1)}, u32[]{:S(2)}) copy-start(f32[5,1024,128]{2,1,0:T(8,128)S(1)} %get-tuple-element.75.cn_near) | copy-start | bytes 7864324
  46.8 26.7 %copy-start.3 = (f32[5,1024,128]{2,1,0:T(8,128)S(1)}, f32[5,1024,128]{2,1,0:T(8,128)}, u32[]{:S(2)}) copy-start(f32[5,1024,128]{2,1,0:T(8,128)} %copy-done.2) | copy-start | bytes 7864324
  46.8 26.7 %copy-start.5 = (f32[4,1024,128]{2,1,0:T(8,128)S(1)}, f32[4,1024,128]{2,1,0:T(8,128)}, u32[]{:S(2)}) copy-start(f32[4,1024,128]{2,1,0:T(8,128)} %copy-done.4) | copy-start | bytes 6291460
  46.8 26.7 %copy-start.7 = (f32[4,1024,128]{2,1,0:T(8,128)S(1)}, f32[4,1024,128]{2,1,0:T(8,128)}, u32[]{:S(2)}) copy-start(f32[4,1024,128]{2,1,0:T(8,128)} %copy-done.6) | copy-start | bytes 6291460
  58.8 5.8 %collective-permute-start.11 = (f32[8,128]{1,0:T(8,128)S(1)}, f32[8,128]{1,0:T(8,128)S(1)}, u32[]{:S(2)}, u32[]{:S(2)}) collective-permute-start(f32[8,128]{1,0:T(8,128)S(1)} %get-tuple-element.67), channel_id=1, source_target_pairs={{0,6},{2,4},{4,2},{6,0},{8,14},{10,12},{12,10},{14,8},{16,22},{18,... | collective-permute-start | bytes 12296 | tf_op jit(solution)/shard_map/ppermute | solution.py:407
  63.6 4.0 %collective-permute-start.10 = (f32[8,128]{1,0:T(8,128)S(1)}, f32[8,128]{1,0:T(8,128)S(1)}, u32[]{:S(2)}, u32[]{:S(2)}) collective-permute-start(f32[8,128]{1,0:T(8,128)S(1)} %get-tuple-element.67), channel_id=1, source_target_pairs={{0,4},{2,6},{4,0},{6,2},{8,12},{10,14},{12,8},{14,10},{16,20},{18,... | collective-permute-start | bytes 12296 | tf_op jit(solution)/shard_map/ppermute | solution.py:407
  63.6 4.0 %collective-permute-start.9 = (f32[8,128]{1,0:T(8,128)S(1)}, f32[8,128]{1,0:T(8,128)S(1)}, u32[]{:S(2)}, u32[]{:S(2)}) collective-permute-start(f32[8,128]{1,0:T(8,128)S(1)} %get-tuple-element.67), channel_id=1, source_target_pairs={{0,2},{2,0},{4,6},{6,4},{8,10},{10,8},{12,14},{14,12},{16,18},{18,... | collective-permute-start | bytes 12296 | tf_op jit(solution)/shard_map/ppermute | solution.py:407
  67.5 3.7 %collective-permute-start.14 = (f32[8,128]{1,0:T(8,128)S(1)}, f32[8,128]{1,0:T(8,128)S(1)}, u32[]{:S(2)}, u32[]{:S(2)}) collective-permute-start(f32[8,128]{1,0:T(8,128)S(1)} %add_add_fusion.3), channel_id=1, source_target_pairs={{0,24},{2,26},{4,28},{6,30},{8,16},{10,18},{12,20},{14,22},{16,8},... | collective-permute-start | bytes 12296 | tf_op jit(solution)/shard_map/ppermute | solution.py:407
  68.8 4.0 %collective-permute-start.13 = (f32[8,128]{1,0:T(8,128)S(1)}, f32[8,128]{1,0:T(8,128)S(1)}, u32[]{:S(2)}, u32[]{:S(2)}) collective-permute-start(f32[8,128]{1,0:T(8,128)S(1)} %add_add_fusion.3), channel_id=1, source_target_pairs={{0,16},{2,18},{4,20},{6,22},{8,24},{10,26},{12,28},{14,30},{16,0},... | collective-permute-start | bytes 12296 | tf_op jit(solution)/shard_map/ppermute | solution.py:407
  70.7 2.8 %collective-permute-start.12 = (f32[8,128]{1,0:T(8,128)S(1)}, f32[8,128]{1,0:T(8,128)S(1)}, u32[]{:S(2)}, u32[]{:S(2)}) collective-permute-start(f32[8,128]{1,0:T(8,128)S(1)} %add_add_fusion.3), channel_id=1, source_target_pairs={{0,8},{2,10},{4,12},{6,14},{8,0},{10,2},{12,4},{14,6},{16,24},{18,... | collective-permute-start | bytes 12296 | tf_op jit(solution)/shard_map/ppermute | solution.py:407
  82.2 3.7 %collective-permute-start.17 = (f32[8,128]{1,0:T(8,128)S(1)}, f32[8,128]{1,0:T(8,128)S(1)}, u32[]{:S(2)}, u32[]{:S(2)}) collective-permute-start(f32[8,128]{1,0:T(8,128)S(1)} %get-tuple-element.76), channel_id=1, source_target_pairs={{0,6},{2,4},{4,2},{6,0},{8,14},{10,12},{12,10},{14,8},{16,22},{18,... | collective-permute-start | bytes 12296 | tf_op jit(solution)/shard_map/ppermute | solution.py:407
  83.6 4.0 %collective-permute-start.16 = (f32[8,128]{1,0:T(8,128)S(1)}, f32[8,128]{1,0:T(8,128)S(1)}, u32[]{:S(2)}, u32[]{:S(2)}) collective-permute-start(f32[8,128]{1,0:T(8,128)S(1)} %get-tuple-element.76), channel_id=1, source_target_pairs={{0,4},{2,6},{4,0},{6,2},{8,12},{10,14},{12,8},{14,10},{16,20},{18,... | collective-permute-start | bytes 12296 | tf_op jit(solution)/shard_map/ppermute | solution.py:407
  84.4 3.2 %collective-permute-start.15 = (f32[8,128]{1,0:T(8,128)S(1)}, f32[8,128]{1,0:T(8,128)S(1)}, u32[]{:S(2)}, u32[]{:S(2)}) collective-permute-start(f32[8,128]{1,0:T(8,128)S(1)} %get-tuple-element.76), channel_id=1, source_target_pairs={{0,2},{2,0},{4,6},{6,4},{8,10},{10,8},{12,14},{14,12},{16,18},{18,... | collective-permute-start | bytes 12296 | tf_op jit(solution)/shard_map/ppermute | solution.py:407
  87.6 4.0 %collective-permute-start.20 = (f32[8,128]{1,0:T(8,128)S(1)}, f32[8,128]{1,0:T(8,128)S(1)}, u32[]{:S(2)}, u32[]{:S(2)}) collective-permute-start(f32[8,128]{1,0:T(8,128)S(1)} %add_add_fusion.1), channel_id=1, source_target_pairs={{0,24},{2,26},{4,28},{6,30},{8,16},{10,18},{12,20},{14,22},{16,8},... | collective-permute-start | bytes 12296 | tf_op jit(solution)/shard_map/ppermute | solution.py:407
  88.4 4.0 %collective-permute-start.19 = (f32[8,128]{1,0:T(8,128)S(1)}, f32[8,128]{1,0:T(8,128)S(1)}, u32[]{:S(2)}, u32[]{:S(2)}) collective-permute-start(f32[8,128]{1,0:T(8,128)S(1)} %add_add_fusion.1), channel_id=1, source_target_pairs={{0,16},{2,18},{4,20},{6,22},{8,24},{10,26},{12,28},{14,30},{16,0},... | collective-permute-start | bytes 12296 | tf_op jit(solution)/shard_map/ppermute | solution.py:407
  89.3 3.1 %collective-permute-start.18 = (f32[8,128]{1,0:T(8,128)S(1)}, f32[8,128]{1,0:T(8,128)S(1)}, u32[]{:S(2)}, u32[]{:S(2)}) collective-permute-start(f32[8,128]{1,0:T(8,128)S(1)} %add_add_fusion.1), channel_id=1, source_target_pairs={{0,8},{2,10},{4,12},{6,14},{8,0},{10,2},{12,4},{14,6},{16,24},{18,... | collective-permute-start | bytes 12296 | tf_op jit(solution)/shard_map/ppermute | solution.py:407
  93.7 13.8 %copy-start.1 = (f32[3,2,128,128]{3,2,1,0:T(8,128)S(1)}, f32[3,2,128,128]{3,2,1,0:T(8,128)}, u32[]{:S(2)}) copy-start(f32[3,2,128,128]{3,2,1,0:T(8,128)} %dual) | copy-start | bytes 1179652
  93.7 7.7 %collective-permute-start.21 = (f32[4,2,128,128]{3,2,1,0:T(8,128)S(1)}, f32[4,2,128,128]{3,2,1,0:T(8,128)S(1)}, u32[]{:S(2)}, u32[]{:S(2)}) collective-permute-start(f32[4,2,128,128]{3,2,1,0:T(8,128)S(1)} %gradient.2), channel_id=1, source_target_pairs={{0,1},{1,0},{2,3},{3,2},{4,5},{5,4},{6,7},{7,6},{8,9},{9,8},{10,11... | collective-permute-start | bytes 1572872 | tf_op jit(solution)/shard_map/ppermute | solution.py:402
  103.5 12.9 %all-to-all-start = ((f32[4,2,128,128]{3,2,1,0:T(8,128)}), f32[4,2,128,128]{3,2,1,0:T(8,128)S(1)}, u32[]{:S(2)}, u32[]{:S(2)}) async-start(f32[4,2,128,128]{3,2,1,0:T(8,128)} %gradient.3), calls=%async_computation | async-start | bytes 1048576 | tf_op jit(solution)/shard_map/all_to_all | solution.py:523
  109.0 19.5 %collective-permute-start.22 = (f32[1,128,128]{2,1,0:T(8,128)S(1)}, f32[1,128,128]{2,1,0:T(8,128)S(1)}, u32[]{:S(2)}, u32[]{:S(2)}) collective-permute-start(f32[1,128,128]{2,1,0:T(8,128)S(1)} %get-tuple-element.89), channel_id=1, source_target_pairs={{0,1},{1,2},{2,3},{3,4},{4,5},{5,6},{6,7},{7,8},{8,9},{9,10},{10,1... | collective-permute-start | bytes 196616 | tf_op jit(solution)/shard_map/ppermute | solution.py:398
  117.2 16.5 %all-to-all-start.1 = ((f32[128,1,128]{2,1,0:T(1,128)}), f32[128,1,128]{2,1,0:T(1,128)S(1)}, u32[]{:S(2)}, u32[]{:S(2)}) async-start(f32[128,1,128]{2,1,0:T(1,128)} %bitcast.13), calls=%async_computation.1 | async-start | bytes 131072 | tf_op jit(solution)/shard_map/all_to_all | solution.py:543
  124.4 4.1 %collective-permute-start.23 = (f32[2,8,128]{2,1,0:T(8,128)S(1)}, f32[2,8,128]{2,1,0:T(8,128)S(1)}, u32[]{:S(2)}, u32[]{:S(2)}) collective-permute-start(f32[2,8,128]{2,1,0:T(8,128)S(1)} %get-tuple-element.90), channel_id=1, source_target_pairs={{0,32},{32,64},{64,96},{1,33},{33,65},{65,97},{2,34},{34,66},{66,9... | collective-permute-start | bytes 24584 | tf_op jit(solution)/shard_map/ppermute | solution.py:398
